TPU v7x, 256 devices: a whole 4x4x8 slice. The times are simulated.
256 devices in a mesh: step: 2 (over core), head: 8 (over z), blk: 16 (over y, x).
Axes of the slice: x: 4, y: 4, z: 8, core: 2. Of those that a mesh axis runs over, the one named last changes fastest.
Arguments:
- states: float32 [2, 2048, 3072], P('step', ('head', 'blk')), may hold values from -6 to 6
- start: float32 [2048, 3072], P(('head', 'blk')), may hold values from -6 to 6
- w_qkv: bfloat16 [3072, 3, 3072], P('blk', None, 'head'), may hold values from -0.109375 to 0.109375
- w_out: bfloat16 [3072, 3072], P(('head', 'blk')), may hold values from -0.109375 to 0.109375
- q_gain: float32 [64], replicated, may hold values from 1.5 to 5
- k_gain: float32 [64], replicated, may hold values from 1.5 to 5
- mod_table: float32 [50, 9216], replicated, may hold values from -3 to 3
- step_index: int32 [2], P('step'), may hold values from 0 to 49
- coef_table: float32 [50], replicated, may hold values from 0.1 to 1
- coef_index: int32 [2], P('step'), may hold values from 0 to 49
Outputs:
- new_states: float32 [2, 2048, 3072], P('step', ('head', 'blk'))
All inputs are finite; a program needn't handle non-finite values.
Results may differ from a plain program's by a relative error of at most 0.008.
Values may be sent and summed in bfloat16 or wider, within the bound.
No kernel may reach another device: no remote copies, remote signals or barrier semaphores. Data moves between devices by JAX's collectives and lax.ppermute only.
A program may use at most 128 MiB of HBM per device.

v0:
```python
import jax
import jax.numpy as jnp
from jax import lax
from jax.sharding import PartitionSpec as P

HD = 64


def carried_in(array, axis, join, neutral):
    place = lax.axis_index(axis)
    gathered = lax.all_gather(array.astype(jnp.bfloat16), axis)
    state = jnp.zeros_like(array) + jnp.asarray(neutral, array.dtype)

    def one(step, state):
        return join(state, lax.dynamic_index_in_dim(gathered, step, 0, False).astype(array.dtype))

    return lax.fori_loop(0, place, one, state)


def head_norm(values_in, gains):
    middle = jnp.mean(values_in, axis=-1, keepdims=True)
    spread = jnp.mean((values_in - middle) ** 2, axis=-1, keepdims=True)
    return (values_in - middle) * lax.rsqrt(spread + 1e-06) * gains


def on_device(
    states, start, w_qkv, w_out, q_gain, k_gain, mod_table, step_index, coef_table, coef_index
):
    width = states.shape[2]
    table_size = mod_table.shape[0]
    slot_ids = jnp.arange(table_size, dtype=jnp.int32)[None, :]
    mod_picks = (step_index[:, None] == slot_ids).astype(jnp.float32)
    coef_picks = (coef_index[:, None] == slot_ids).astype(jnp.float32)
    modulation = jnp.dot(mod_picks, mod_table, precision=lax.Precision.HIGHEST).reshape(
        -1, 3, width
    )
    coefs = jnp.sum(coef_picks * coef_table[None, :], axis=1)
    middle = jnp.mean(states, axis=-1, keepdims=True)
    spread = jnp.mean((states - middle) ** 2, axis=-1, keepdims=True)
    normed = (
        (states - middle) * lax.rsqrt(spread + 1e-05) * (1.0 + modulation[:, 1][:, None, :])
        + modulation[:, 0][:, None, :]
    ).astype(jnp.bfloat16)
    weight_rows = lax.all_gather(w_qkv, "blk", axis=0, tiled=True)
    projected = jnp.einsum(
        "std,dce->stce",
        lax.all_gather(normed, "head", axis=1, tiled=True),
        weight_rows,
        preferred_element_type=jnp.float32,
    )
    step_count = projected.shape[0]
    row_count = projected.shape[1]
    local_heads = projected.shape[3] // HD
    queries = head_norm(
        projected[:, :, 0].reshape(step_count, row_count, local_heads, HD), q_gain
    ).astype(jnp.bfloat16)
    keys_here = head_norm(
        projected[:, :, 1].reshape(step_count, row_count, local_heads, HD), k_gain
    ).astype(jnp.bfloat16)
    values_here = (
        projected[:, :, 2].reshape(step_count, row_count, local_heads, HD).astype(jnp.bfloat16)
    )
    scale_factor = HD ** (-0.5)
    start_best = jnp.full((step_count, local_heads, row_count), -1e30, jnp.float32)
    start_totals = jnp.zeros((step_count, local_heads, row_count), jnp.float32)
    start_accum = jnp.zeros((step_count, local_heads, row_count, HD), jnp.float32)
    best = start_best
    totals = start_totals
    accum = start_accum
    key_piece = lax.all_gather(keys_here, "blk", axis=1, tiled=True)
    value_piece = lax.all_gather(values_here, "blk", axis=1, tiled=True)
    length = key_piece.shape[1]
    for offset in range(0, length, 512):
        stop = min(offset + 512, length)
        key_block = key_piece[:, offset:stop]
        value_block = value_piece[:, offset:stop]
        scores = (
            jnp.einsum("sqhd,skhd->shqk", queries, key_block, preferred_element_type=jnp.float32)
            * scale_factor
        )
        new_best = jnp.maximum(best, jnp.max(scores, axis=-1))
        factor = jnp.exp(best - new_best)
        weights = jnp.exp(scores - new_best[..., None])
        totals = totals * factor + jnp.sum(weights, axis=-1)
        accum = accum * factor[..., None] + jnp.einsum(
            "shqk,skhd->shqd",
            weights.astype(jnp.bfloat16),
            value_block,
            preferred_element_type=jnp.float32,
        )
        best = new_best
    best, totals, accum = (best, totals, accum)
    attn = jnp.transpose(accum / totals[..., None], (0, 2, 1, 3)).reshape(
        step_count, row_count, local_heads * HD
    )
    attn = attn.astype(jnp.bfloat16)
    group_terms = jnp.einsum(
        "srf,fe->sre",
        attn,
        lax.all_gather(w_out, "blk", axis=0, tiled=True),
        preferred_element_type=jnp.float32,
    )
    mixed = lax.psum_scatter(
        group_terms.astype(jnp.bfloat16), "head", scatter_dimension=1, tiled=True
    ).astype(jnp.float32)
    drift = modulation[:, 2][:, None, :] * mixed
    inclusive = jnp.cumsum(coefs[:, None, None] * drift, axis=0)
    own_total = inclusive[-1]
    earlier = carried_in(
        own_total, "step", lambda first, second: first + second, jnp.zeros_like(own_total)
    )
    return start[None] + (earlier[None] + inclusive)


def solution(mesh):
    in_specs = (
        P("step", ("head", "blk"), None),
        P(("head", "blk"), None),
        P("blk", None, "head"),
        P(("head", "blk"), None),
        P(),
        P(),
        P(),
        P("step"),
        P(),
        P("step"),
    )
    out_specs = P("step", ("head", "blk"), None)
    return jax.shard_map(
        on_device, mesh=mesh, in_specs=in_specs, out_specs=out_specs, check_vma=False
    )
```

profile of v0, /device:TPU:1, one launch (start us, length us, event | category | flops | bytes accessed | tf_op | source)
XLA Modules:
  0.0 296.6 jit_solution(17532198144011052119)
XLA Ops:
  6.5 0.0 all-gather.5.cloned.1.call-start
  6.5 0.7 all-gather.5.cloned.1.call-update
  7.3 0.0 all-gather.7.cloned.1.call-start
  7.3 0.0 copy-start.3
  7.3 3.2 %reshape.440 = f32[3,3072,50]{1,0,2:T(4,128)S(1)} reshape(f32[9216,50]{0,1:T(8,128)} %bitcast.98) | data formatting | bytes 3686400 | tf_op jit(solution)/shard_map/reshape.224
  11.1 0.0 copy-done.3
  11.2 0.1 reduce_sum.100
  11.3 0.2 multiply_reduce_fusion.2
  11.5 1.8 fusion.1
  13.4 0.1 add_convert_fusion
  13.5 25.1 %all_gather.19 = bf16[1,128,3072]{2,1,0:T(8,128)(2,1)S(1)} all-gather(bf16[1,16,3072]{2,1,0:T(8,128)(2,1)S(1)} %add_convert_fusion), channel_id=1, replica_groups=mesh['step'=2,'head'=8,'blk'=16] {'head'}, dimensions={1}, use_global_device_ids=true | all-gather | bytes 884736 | tf_op jit(solution)/shard_map/all_gather | solution.py:47
  38.6 45.0 %all-gather.5.cloned.1.call-done = bf16[3072,3,384]{2,0,1:T(8,128)(2,1)} async-done(((bf16[192,3,384]{2,0,1:T(8,128)(2,1)}), bf16[3072,3,384]{2,0,1:T(8,128)(2,1)}) %all-gather.5.cloned.1.call-update) | async-done | bytes 7077904 | tf_op jit(solution)/shard_map/all_gather | solution.py:44
  83.5 4.2 %convolution_bitcast_fusion = f32[1,128,3,384]{3,1,2,0:T(8,128)S(1)} fusion(bf16[3072,3,384]{2,0,1:T(8,128)(2,1)} %all-gather.5.cloned.1.call-done, bf16[1,128,3072]{2,1,0:T(8,128)(2,1)S(1)} %all_gather.19), kind=kOutput, calls=%fused_computation.21 | convolution fusion | flops 905969664 | bytes 8454144 | tf_op jit(solution)/shard_map/std,dce->stce/dot_general | solution.py:45
  87.8 0.0 copy-start.8
  87.8 0.0 copy-start.9
  87.8 0.1 copy.22
  88.0 0.4 copy-done.8
  88.4 0.7 multiply_convert_fusion
  89.1 0.0 all-gather.7.cloned.1.call-update
  89.2 0.0 all-gather.9.cloned.1.call-start
  89.2 0.7 copy.24
  90.0 0.0 all-gather.9.cloned.1.call-update
  90.0 0.0 all-gather.11.cloned.1.call-start
  90.0 0.5 all-gather.11.cloned.1.call-update
  90.6 0.0 reduce-scatter.2.cloned.1.call-start
  90.6 0.1 copy.20
  90.8 0.0 copy-done.9
  90.9 0.1 multiply_convert_fusion.1
  90.9 47.2 %all-gather.7.cloned.1.call-done = bf16[1,2048,6,64]{1,3,2,0:T(8,128)(2,1)} async-done(((bf16[1,128,6,64]{1,3,2,0:T(8,128)(2,1)}), bf16[1,2048,6,64]{1,3,2,0:T(8,128)(2,1)}) %all-gather.7.cloned.1.call-update) | async-done | bytes 1572880 | tf_op jit(solution)/shard_map/all_gather | solution.py:70
  138.2 0.0 copy-start.4
  138.2 1.6 fusion.41
  139.8 0.0 copy-done.4
  139.8 0.0 copy-start
  139.8 0.5 fusion.40
  140.3 0.5 fusion.39
  140.8 0.5 fusion.38
  141.3 0.0 copy-start.1
  141.3 0.0 copy-done
  141.3 0.9 fusion.3
  142.2 0.2 copy-done.1
  142.5 0.9 fusion.7
  143.4 47.1 %all-gather.9.cloned.1.call-done = bf16[1,2048,6,64]{1,3,2,0:T(8,128)(2,1)} async-done(((bf16[1,128,6,64]{1,3,2,0:T(8,128)(2,1)}), bf16[1,2048,6,64]{1,3,2,0:T(8,128)(2,1)}) %all-gather.9.cloned.1.call-update) | async-done | bytes 1572880 | tf_op jit(solution)/shard_map/all_gather | solution.py:71
  190.5 0.0 copy-start.5
  190.5 2.1 fusion.14
  192.5 0.0 copy-done.5
  192.5 0.5 fusion.13
  193.0 0.0 copy-start.2
  193.0 0.5 fusion.12
  193.5 0.9 copy-done.2
  194.4 0.5 fusion.15
  194.9 48.3 %all-gather.11.cloned.1.call-done = bf16[384,3072]{1,0:T(8,128)(2,1)} async-done(((bf16[24,3072]{1,0:T(8,128)(2,1)}), bf16[384,3072]{1,0:T(8,128)(2,1)}) %all-gather.11.cloned.1.call-update) | async-done | bytes 2359312 | tf_op jit(solution)/shard_map/all_gather | solution.py:100
  243.3 3.2 %fusion = bf16[1,128,3072]{2,1,0:T(8,128)(2,1)} fusion(bf16[128,384]{0,1:T(8,128)(2,1)S(1)} %bitcast.102, bf16[384,3072]{1,0:T(8,128)(2,1)} %all-gather.11.cloned.1.call-done), kind=kOutput, calls=%fused_computation.2 | convolution fusion | flops 302383104 | bytes 3244032 | tf_op jit(solution)/shard_map/srf,fe->sre/dot_general | solution.py:97
  246.4 0.0 reduce-scatter.2.cloned.1.call-update
  247.1 0.0 copy-done.10
  247.1 0.6 fusion.30
  247.7 32.7 %reduce-scatter.2.cloned.1.call-done = bf16[1,16,3072]{2,1,0:T(8,128)(2,1)} async-done(((bf16[1,128,3072]{2,1,0:T(8,128)(2,1)}), bf16[1,16,3072]{2,1,0:T(8,128)(2,1)}) %reduce-scatter.2.cloned.1.call-update) | async-done | bytes 98320 | tf_op jit(solution)/shard_map/reduce_scatter | solution.py:103
  280.4 1.5 fusion.26
  281.9 0.0 copy-start.6
  281.9 0.0 copy-start.7
  281.9 6.8 %all_gather.24 = bf16[2,16,3072]{2,1,0:T(8,128)(2,1)S(1)} all-gather(bf16[1,16,3072]{2,1,0:T(8,128)(2,1)S(1)} %fusion.26), channel_id=1, replica_groups=mesh['step'=2,'head'=8,'blk'=16] {'step'}, dimensions={0}, use_global_device_ids=true | all-gather | bytes 294912 | tf_op jit(solution)/shard_map/all_gather | solution.py:11
  288.7 0.1 while.10
  288.8 0.0 copy-done.6
  288.8 0.0 copy-done.7
  288.8 1.3 fusion.25
  (19 shorter events, 0.3 us)
Async XLA Ops:
  6.5 77.0 %all-gather.5.cloned.1.call-start = ((), (), s32[]{:S(2)}) async-start(), calls=%async_computation.1 | async-start | bytes 7520256 | tf_op jit(solution)/shard_map/all_gather | solution.py:44
  7.3 130.9 %all-gather.7.cloned.1.call-start = ((), (), s32[]{:S(2)}) async-start(), calls=%async_computation.2 | async-start | bytes 1671168 | tf_op jit(solution)/shard_map/all_gather | solution.py:70
  7.3 3.8 %copy-start.3 = (f32[1,16,3072]{2,1,0:T(8,128)S(1)}, f32[1,16,3072]{2,1,0:T(8,128)}, u32[]{:S(2)}) copy-start(f32[1,16,3072]{2,1,0:T(8,128)} %param.12) | copy-start | bytes 589828
  87.8 0.7 copy-start.8
  87.8 3.1 %copy-start.9 = (f32[64]{0:T(128)S(1)}, f32[64]{0:T(128)}, u32[]{:S(2)}) copy-start(f32[64]{0:T(128)} %param.16) | copy-start | bytes 772
  89.2 101.3 %all-gather.9.cloned.1.call-start = ((), (), s32[]{:S(2)}) async-start(), calls=%async_computation.3 | async-start | bytes 1671168 | tf_op jit(solution)/shard_map/all_gather | solution.py:71
  90.0 153.3 %all-gather.11.cloned.1.call-start = ((), (), s32[]{:S(2)}) async-start(), calls=%async_computation.4 | async-start | bytes 2506752 | tf_op jit(solution)/shard_map/all_gather | solution.py:100
  90.6 189.8 %reduce-scatter.2.cloned.1.call-start = ((), (), s32[]{:S(2)}) async-start(), calls=%async_computation.5 | async-start | bytes 884736 | tf_op jit(solution)/shard_map/reduce_scatter | solution.py:103
  138.2 1.6 copy-start.4
  139.8 1.5 copy-start
  141.3 1.2 copy-start.1
  190.5 2.1 copy-start.5
  193.0 1.4 copy-start.2
  243.3 3.9 %copy-start.10 = (f32[50]{0:T(128)S(1)}, f32[50]{0:T(128)}, u32[]{:S(2)}) copy-start(f32[50]{0:T(128)} %param.20) | copy-start | bytes 604
  281.9 6.9 %copy-start.6 = (bf16[1,16,3072]{2,1,0:T(8,128)(2,1)S(1)}, bf16[1,16,3072]{2,1,0:T(8,128)(2,1)}, u32[]{:S(2)}) copy-start(bf16[1,16,3072]{2,1,0:T(8,128)(2,1)} %reduce-scatter.2.cloned.1.call-done) | copy-start | bytes 294916
  281.9 6.9 %copy-start.7 = (f32[16,3072]{1,0:T(8,128)S(1)}, f32[16,3072]{1,0:T(8,128)}, u32[]{:S(2)}) copy-start(f32[16,3072]{1,0:T(8,128)} %param.13) | copy-start | bytes 589828
Sparse Core Ops, SparseCore 0:
  9.8 73.7 all-gather.4
  89.3 48.8 all-gather.6
  140.6 49.8 all-gather.8
  192.8 50.4 all-gather.10
  246.6 33.7 reduce-scatter.1
where the time goes:
time: 297 us
  waiting for transfers between devices  222 us (75%)
  blocking collectives  31.8 us (11%)
  matrix products  15.8 us (5%)
  between operations  14.8 us (5%)
  other arithmetic  6.61 us (2%)
  local copies, waits for them, and re-layouts  5.77 us (2%)
    all_gather x1, waiting for transfers between devices, on_device(): lax.all_gather(w_out, 'blk', axis=0, tiled=True)  48.3 us
    all_gather x1, waiting for transfers between devices, on_device(): key_piece = lax.all_gather(keys_here, 'blk', axis=1, tiled=True)  47.2 us
    all_gather x1, waiting for transfers between devices, on_device(): value_piece = lax.all_gather(values_here, 'blk', axis=1, tiled=True)  47.1 us
    all_gather x1, waiting for transfers between devices, on_device(): weight_rows = lax.all_gather(w_qkv, 'blk', axis=0, tiled=True)  45 us
    reduce_scatter x1, waiting for transfers between devices, on_device(): lax.psum_scatter(group_terms.astype(jnp.bfloat16), 'head', scatter_dimens...  32.7 us
    all_gather x1, blocking collectives, on_device(): lax.all_gather(normed, 'head', axis=1, tiled=True)  25.1 us
    all_gather x1, blocking collectives, carried_in(): gathered = lax.all_gather(array.astype(jnp.bfloat16), axis)  6.76 us
  transfers between devices with their start and end apart: 5, of which 5 were waited for; matrix products, arithmetic and copies ran while one was open for 5% of the time, Pallas kernels for 0%

commit v1 on v0

v1 whole, which is shorter than its diff:
```python
import jax
import jax.numpy as jnp
from jax import lax
from jax.experimental import pallas as pl
from jax.experimental.pallas import tpu as pltpu
from jax.sharding import Mesh, PartitionSpec as P

HD = 64
BF = jnp.bfloat16
F32 = jnp.float32


def shift_pairs(size, offset):
    return [(i, (i - offset) % size) for i in range(size)]


def head_norm(values_in, gains):
    middle = jnp.mean(values_in, axis=-1, keepdims=True)
    spread = jnp.mean((values_in - middle) ** 2, axis=-1, keepdims=True)
    return (values_in - middle) * lax.rsqrt(spread + 1e-06) * gains


def ring_of_four(block, axis):
    after = lax.ppermute(block, axis, shift_pairs(4, 1))
    before = lax.ppermute(block, axis, shift_pairs(4, 3))
    across = lax.ppermute(block, axis, shift_pairs(4, 2))
    return jnp.stack([block, after, across, before])


def ring_forwarded(block, axis):
    after = lax.ppermute(block, axis, shift_pairs(4, 1))
    before = lax.ppermute(block, axis, shift_pairs(4, 3))
    half = block.shape[0] // 2
    low = lax.ppermute(after[:half], axis, shift_pairs(4, 1))
    high = lax.ppermute(before[half:], axis, shift_pairs(4, 3))
    return [block, after, before, low, high]


def attention_kernel(q_ref, kv_ref, o_ref):
    lane = lax.broadcasted_iota(jnp.int32, (1, 128), 1)
    low = lane < 64
    dims = (((1,), (1,)), ((), ()))

    def head(q_tile, k_tile, v_tile):
        scores = lax.dot_general(q_tile, k_tile, dims, preferred_element_type=F32)
        peak = jnp.max(scores, axis=-1, keepdims=True)
        weights = jnp.exp(scores - peak)
        total = jnp.sum(weights, axis=-1, keepdims=True)
        mixed = jnp.dot(weights.astype(BF), v_tile, preferred_element_type=F32)
        return mixed / total

    pair = q_ref[:, 0:128]
    zero = jnp.zeros_like(pair)
    tile_a, tile_b, tile_c = kv_ref[:, 0:128], kv_ref[:, 128:256], kv_ref[:, 256:384]
    first = head(jnp.where(low, pair, zero), tile_b, tile_c)
    second = head(jnp.where(low, zero, pair), tile_b, tile_c)
    o_ref[:, 0:128] = jnp.where(low, first, second).astype(o_ref.dtype)
    third = head(q_ref[:, 128:256], tile_a, tile_a)
    o_ref[:, 128:192] = third[:, 0:64].astype(o_ref.dtype)


def attention(q, kv):
    rows = q.shape[0]
    vmem = pl.BlockSpec(memory_space=pltpu.VMEM)
    return pl.pallas_call(
        attention_kernel,
        out_shape=jax.ShapeDtypeStruct((rows, 192), BF),
        in_specs=[vmem, vmem],
        out_specs=vmem,
        compiler_params=pltpu.CompilerParams(vmem_limit_bytes=40 * 1024 * 1024),
        cost_estimate=pl.CostEstimate(
            flops=4 * rows * kv.shape[0] * 3 * 128,
            bytes_accessed=kv.size * 2,
            transcendentals=rows * kv.shape[0] * 3,
        ),
    )(q, kv)


def on_device(
    states, start, w_qkv, w_out, q_gain, k_gain, mod_table, step_index, coef_table, coef_index
):
    width = states.shape[2]
    tokens = states.shape[1]
    half = width // 2
    core = lax.axis_index("c")
    at_y = lax.axis_index("y")
    at_x = lax.axis_index("x")
    first_core = core == 0
    swap = [(0, 1), (1, 0)]
    x_pairs = [(i, i ^ 1) for i in range(4)]
    diagonal = [(i, i ^ 5) for i in range(8)]

    w_core = lax.dynamic_slice_in_dim(w_qkv, core * 192, 192, axis=2).reshape(192, 576)
    by_x = ring_of_four(w_core[:96], "x")
    by_y = ring_of_four(w_core[96:], "y")
    pieces = ring_forwarded(by_x, "y") + ring_forwarded(by_y, "x")
    weights = jnp.concatenate([p.reshape(-1, 576) for p in pieces], axis=0)

    w_out_half = lax.dynamic_slice_in_dim(w_out, core * half, half, axis=1)
    w_out_rows = lax.all_gather(w_out_half, ("y", "x"), axis=0, tiled=True)

    own_index = jnp.concatenate([step_index, coef_index])
    other_index = lax.ppermute(own_index, "c", swap)
    first_index = jnp.where(first_core, own_index, other_index)
    second_index = jnp.where(first_core, other_index, own_index)

    row = lax.dynamic_index_in_dim(mod_table, step_index[0], 0, True)
    current = states[0]
    middle = jnp.mean(current, axis=-1, keepdims=True)
    spread = jnp.mean((current - middle) ** 2, axis=-1, keepdims=True)
    normed = (
        (current - middle) * lax.rsqrt(spread + 1e-05) * (1.0 + row[:, width : 2 * width])
        + row[:, :width]
    ).astype(BF)
    blocks = normed.reshape(tokens, 4, 4, 192)
    blocks = lax.dynamic_slice_in_dim(jnp.concatenate([blocks, blocks], axis=1), at_y, 4, axis=1)
    blocks = lax.dynamic_slice_in_dim(jnp.concatenate([blocks, blocks], axis=2), at_x, 4, axis=2)
    order = [0, 1, 3, 2]
    part_x = jnp.concatenate([blocks[:, i : i + 1, :, :96] for i in order], axis=1)
    part_y = jnp.concatenate([blocks[:, :, i : i + 1, 96:] for i in order], axis=2)
    arranged = jnp.concatenate(
        [part_x.reshape(tokens, half), jnp.swapaxes(part_y, 1, 2).reshape(tokens, half)], axis=1
    )
    theirs = lax.ppermute(arranged, "c", swap)
    both = jnp.where(
        first_core, jnp.stack([arranged, theirs]), jnp.stack([theirs, arranged])
    )
    gathered = lax.all_gather(both, "z", axis=0, tiled=False)
    groups = gathered.shape[0]
    rows = groups * tokens

    projected = jnp.dot(
        gathered.reshape(2 * rows, width), weights, preferred_element_type=F32
    ).reshape(groups, 2, tokens, 3, 3, HD)
    projected = jnp.swapaxes(projected, 0, 1).reshape(2, rows, 3, 3, HD)
    queries = (head_norm(projected[:, :, 0], q_gain).astype(BF) * BF(HD**-0.5)).reshape(2, rows, 192)
    keys = head_norm(projected[:, :, 1], k_gain).astype(BF).reshape(2, rows, 192)
    values = projected[:, :, 2].astype(BF).reshape(2, rows, 192)
    queries = jnp.concatenate(
        [queries[..., :128], jnp.zeros_like(queries[..., :64]), queries[..., 128:]], axis=-1
    )
    keys_values = jnp.concatenate(
        [values[..., 128:], keys[..., 128:], keys[..., :128], values[..., :128]], axis=-1
    )

    step = at_x % 2
    first_step = step == 0
    q_kept = jnp.where(first_step, queries[0], queries[1])
    q_given = jnp.where(first_step, queries[1], queries[0])
    q_got = lax.ppermute(q_given, "x", x_pairs)
    outgoing = jnp.broadcast_to(keys_values[None], (8, 2, rows, 384)).reshape(16, rows, 384)
    incoming = lax.all_to_all(outgoing, ("y", "x"), 0, 0, tiled=True)
    attn = attention(jnp.concatenate([q_kept, q_got], axis=0), incoming.reshape(16 * rows, 384))

    mine, partners = attn[:rows], attn[rows:]
    mine_core = lax.ppermute(mine, "c", swap)
    here = lax.ppermute(partners, "x", x_pairs)
    here_core = lax.ppermute(partners, ("c", "x"), diagonal)

    def heads_in_order(own, other):
        return jnp.where(
            first_core,
            jnp.concatenate([own, other], axis=1),
            jnp.concatenate([other, own], axis=1),
        )

    this_step, that_step = heads_in_order(mine, mine_core), heads_in_order(here, here_core)
    features = jnp.where(
        first_step, jnp.stack([this_step, that_step]), jnp.stack([that_step, this_step])
    )
    features = jnp.swapaxes(features.reshape(2, groups, tokens, 384), 0, 1)
    share = jnp.dot(
        features.reshape(2 * rows, 384), w_out_rows, preferred_element_type=F32
    ).astype(BF)
    arrived = lax.all_to_all(share.reshape(groups, 2 * tokens, half), "z", 0, 0, tiled=True)
    mixed = jnp.sum(arrived.astype(F32), axis=0).reshape(2, tokens, half)

    def weighted(index, drift):
        gate = lax.dynamic_slice(mod_table, (index[0], 2 * width + core * half), (1, half))
        return coef_table[index[1]] * (gate * drift)

    first = weighted(first_index, mixed[0])
    second = first + weighted(second_index, mixed[1])
    kept = jnp.where(first_core, first, second)
    given = jnp.where(first_core, second, first)
    got = lax.ppermute(given, "c", swap)
    moved = jnp.where(
        first_core,
        jnp.concatenate([kept, got], axis=1),
        jnp.concatenate([got, kept], axis=1),
    )
    return (start + moved)[None]


def solution(mesh):
    grid = Mesh(mesh.devices.reshape(2, 8, 4, 4), ("c", "z", "y", "x"))
    tokens = ("z", "y", "x")
    in_specs = (
        P("c", tokens, None),
        P(tokens, None),
        P(("y", "x"), None, "z"),
        P(tokens, None),
        P(),
        P(),
        P(),
        P("c"),
        P(),
        P("c"),
    )
    return jax.shard_map(
        on_device, mesh=grid, in_specs=in_specs, out_specs=P("c", tokens, None), check_vma=False
    )
```

time: 297 us -> 161 us (0.54)
  waiting for transfers between devices: 222 us -> 52.4 us
  starting transfers between devices: 0.16 us -> 44.3 us
  blocking collectives: 31.8 us -> 0 us
  local copies, waits for them, and re-layouts: 5.77 us -> 22.4 us
  matrix products: 15.8 us -> 7.41 us
  between operations: 14.8 us -> 22.9 us
    all_gather x4 -> x2, waiting for transfers between devices: 188 us -> 5.51 us  [the longest x1 5.51 us: on_device(): w_out_rows = lax.all_gather(w_out_half, ('y', 'x'), axis=0, tiled=True)]
    ppermute x0 -> x21, waiting for transfers between devices: none -> 37 us  [the longest x1 17.4 us: on_device(): q_got = lax.ppermute(q_given, 'x', x_pairs)]
    ppermute x0 -> x21, starting transfers between devices: none -> 33.4 us  [the longest x2 5.19 us: ring_forwarded(): low = lax.ppermute(after[:half], axis, shift_pairs(4, 1))]
    reduce_scatter x1 -> x0, waiting for transfers between devices: 32.7 us -> none  [on_device(): lax.psum_scatter(group_terms.astype(jnp.bfloat16), 'head', scatter_dimens...]
    all_gather x2 -> x0, blocking collectives: 31.8 us -> none  [the longest x1 25.1 us: on_device(): lax.all_gather(normed, 'head', axis=1, tiled=True)]
    all_to_all x0 -> x2, starting transfers between devices: none -> 10.8 us  [the longest x1 7.09 us: on_device(): lax.all_to_all(share.reshape(groups, 2 * tokens, half), 'z', 0, 0, tiled=...]
    all_to_all x0 -> x2, waiting for transfers between devices: none -> 9.83 us  [the longest x1 8.5 us: on_device(): lax.all_to_all(share.reshape(groups, 2 * tokens, half), 'z', 0, 0, tiled=...]
    dot_general x11 -> x2, matrix products: 15.8 us -> 7.41 us  [the longest x1 4.68 us: on_device(): jnp.dot(gathered.reshape(2 * rows, width), weights, preferred_element_typ...]
  transfers between devices with their start and end apart: 5 -> 25, of which waited for: 5 -> 14; matrix products, arithmetic and copies ran while one was open for 5% -> 17% of each run, Pallas kernels for 0% -> 2%
where the time goes in v1:
time: 161 us
  waiting for transfers between devices  52.4 us (33%)
  starting transfers between devices  44.3 us (28%)
  between operations  22.9 us (14%)
  local copies, waits for them, and re-layouts  22.4 us (14%)
  other arithmetic  8.79 us (5%)
  matrix products  7.41 us (5%)
  Pallas kernels  2.57 us (2%)
    ppermute x1, waiting for transfers between devices, on_device(): q_got = lax.ppermute(q_given, 'x', x_pairs)  17.4 us
    all_to_all x1, waiting for transfers between devices, on_device(): lax.all_to_all(share.reshape(groups, 2 * tokens, half), 'z', 0, 0, tiled=...  8.5 us
    unnamed x22, local copies, waits for them, and re-layouts  7.23 us
    all_to_all x1, starting transfers between devices, on_device(): lax.all_to_all(share.reshape(groups, 2 * tokens, half), 'z', 0, 0, tiled=...  7.09 us
    dot_general x1, local copies, waits for them, and re-layouts, on_device(): jnp.dot(gathered.reshape(2 * rows, width), weights, preferred_element_typ...  5.96 us
    ppermute x2, waiting for transfers between devices, ring_forwarded(): after = lax.ppermute(block, axis, shift_pairs(4, 1))  5.56 us
    all_gather x1, waiting for transfers between devices, on_device(): w_out_rows = lax.all_gather(w_out_half, ('y', 'x'), axis=0, tiled=True)  5.51 us
    ppermute x2, starting transfers between devices, ring_forwarded(): low = lax.ppermute(after[:half], axis, shift_pairs(4, 1))  5.19 us
  transfers between devices with their start and end apart: 25, of which 14 were waited for; matrix products, arithmetic and copies ran while one was open for 17% of the time, Pallas kernels for 2%

profile of v1, /device:TPU:1, one launch (start us, length us, event | category | flops | bytes accessed | tf_op | source)
XLA Modules:
  0.0 160.8 jit_solution(15238895183059212742)
XLA Ops:
  7.3 1.1 fusion.24
  8.5 1.1 squeeze.46
  9.6 1.1 reduce_sum.63
  10.7 1.1 fusion.18
  12.0 0.3 fusion.21
  12.3 0.2 fusion.20
  13.4 3.3 %collective-permute-start.1 = (bf16[16,3072]{1,0:T(8,128)(2,1)S(1)}, bf16[16,3072]{1,0:T(8,128)(2,1)S(1)}, u32[]{:S(2)}, u32[]{:S(2)}) collective-permute-start(bf16[16,3072]{1,0:T(8,128)(2,1)S(1)} %constant_dynamic-update-slice_fusion), channel_id=1, source_target_pairs={{0,128},{128,0},{1,129},{129,1},{2,130},{130,2},{3,131},{131,3},{4... | collective-permute-start | bytes 294920 | tf_op jit(solution)/shard_map/ppermute | solution.py:124
  16.7 0.9 collective-permute-done.1
  17.7 0.7 maximum_select_fusion
  18.8 0.8 collective-permute-start.2
  19.6 0.5 collective-permute-start.3
  20.2 0.6 collective-permute-start.4
  20.9 2.8 %collective-permute-start.9 = (bf16[96,576]{0,1:T(8,128)(2,1)S(1)}, bf16[96,576]{0,1:T(8,128)(2,1)S(1)}, u32[]{:S(2)}, u32[]{:S(2)}) collective-permute-start(bf16[96,576]{0,1:T(8,128)(2,1)S(1)} %bitcast.130), channel_id=1, source_target_pairs={{0,12},{4,0},{8,4},{12,8},{1,13},{5,1},{9,5},{13,9},{2,14},{6,2},{... | collective-permute-start | bytes 331784 | tf_op jit(solution)/shard_map/ppermute | solution.py:24
  23.7 0.3 collective-permute-start.10
  24.1 2.7 %collective-permute-start.11 = (bf16[96,576]{0,1:T(8,128)(2,1)S(1)}, bf16[96,576]{0,1:T(8,128)(2,1)S(1)}, u32[]{:S(2)}, u32[]{:S(2)}) collective-permute-start(bf16[96,576]{0,1:T(8,128)(2,1)S(1)} %bitcast.132), channel_id=1, source_target_pairs={{0,4},{4,8},{8,12},{12,0},{1,5},{5,9},{9,13},{13,1},{2,6},{6,10},{... | collective-permute-start | bytes 331784 | tf_op jit(solution)/shard_map/ppermute | solution.py:25
  26.8 3.2 %collective-permute-done.4 = bf16[96,576]{0,1:T(8,128)(2,1)S(1)} collective-permute-done((bf16[96,576]{0,1:T(8,128)(2,1)S(1)}, bf16[96,576]{0,1:T(8,128)(2,1)S(1)}, u32[]{:S(2)}, u32[]{:S(2)}) %collective-permute-start.4) | collective-permute-done | bytes 110624 | tf_op jit(solution)/shard_map/ppermute | solution.py:25
  30.2 0.3 copy.105
  30.5 2.8 %collective-permute-start.5 = (bf16[4,96,576]{2,1,0:T(8,128)(2,1)S(1)}, bf16[4,96,576]{2,1,0:T(8,128)(2,1)S(1)}, u32[]{:S(2)}, u32[]{:S(2)}) collective-permute-start(bf16[4,96,576]{2,1,0:T(8,128)(2,1)S(1)} %copy.105), channel_id=1, source_target_pairs={{0,12},{4,0},{8,4},{12,8},{1,13},{5,1},{9,5},{13,9},{2,14},{6,2},{... | collective-permute-start | bytes 1327112 | tf_op jit(solution)/shard_map/ppermute | solution.py:31
  33.3 0.3 collective-permute-done.11
  33.8 0.3 copy.112
  34.1 2.2 %collective-permute-start.12 = (bf16[4,96,576]{2,1,0:T(8,128)(2,1)S(1)}, bf16[4,96,576]{2,1,0:T(8,128)(2,1)S(1)}, u32[]{:S(2)}, u32[]{:S(2)}) collective-permute-start(bf16[4,96,576]{2,1,0:T(8,128)(2,1)S(1)} %copy.112), channel_id=1, source_target_pairs={{0,3},{1,0},{2,1},{3,2},{4,7},{5,4},{6,5},{7,6},{8,11},{9,8},{10,9... | collective-permute-start | bytes 1327112 | tf_op jit(solution)/shard_map/ppermute | solution.py:31
  36.3 0.6 constant_dynamic-slice_fusion
  37.0 0.8 constant_dynamic-update-slice_fusion.11
  37.9 5.6 %collective-permute-done.5 = bf16[4,96,576]{2,1,0:T(8,128)(2,1)S(1)} collective-permute-done((bf16[4,96,576]{2,1,0:T(8,128)(2,1)S(1)}, bf16[4,96,576]{2,1,0:T(8,128)(2,1)S(1)}, u32[]{:S(2)}, u32[]{:S(2)}) %collective-permute-start.5) | collective-permute-done | bytes 442400 | tf_op jit(solution)/shard_map/ppermute | solution.py:31
  43.4 3.5 %collective-permute-start.7 = (bf16[2,96,576]{2,1,0:T(8,128)(2,1)S(1)}, bf16[2,96,576]{2,1,0:T(8,128)(2,1)S(1)}, u32[]{:S(2)}, u32[]{:S(2)}) collective-permute-start(bf16[2,96,576]{2,1,0:T(8,128)(2,1)S(1)} %slice.155), channel_id=1, source_target_pairs={{0,12},{4,0},{8,4},{12,8},{1,13},{5,1},{9,5},{13,9},{2,14},{6,2},{... | collective-permute-start | bytes 663560 | tf_op jit(solution)/shard_map/ppermute | solution.py:34
  47.0 0.3 collective-permute-start.8
  47.3 1.7 %collective-permute-start.14 = (bf16[2,96,576]{2,1,0:T(8,128)(2,1)S(1)}, bf16[2,96,576]{2,1,0:T(8,128)(2,1)S(1)}, u32[]{:S(2)}, u32[]{:S(2)}) collective-permute-start(bf16[2,96,576]{2,1,0:T(8,128)(2,1)S(1)} %slice.157), channel_id=1, source_target_pairs={{0,3},{1,0},{2,1},{3,2},{4,7},{5,4},{6,5},{7,6},{8,11},{9,8},{10,9... | collective-permute-start | bytes 663560 | tf_op jit(solution)/shard_map/ppermute | solution.py:34
  49.1 0.8 constant_dynamic-update-slice_fusion.10
  49.9 0.8 constant_dynamic-update-slice_fusion.9
  50.9 0.7 constant_dynamic-update-slice_fusion.8
  51.6 2.7 %collective-permute-done.8 = bf16[2,96,576]{2,1,0:T(8,128)(2,1)S(1)} collective-permute-done((bf16[2,96,576]{2,1,0:T(8,128)(2,1)S(1)}, bf16[2,96,576]{2,1,0:T(8,128)(2,1)S(1)}, u32[]{:S(2)}, u32[]{:S(2)}) %collective-permute-start.8) | collective-permute-done | bytes 221216 | tf_op jit(solution)/shard_map/ppermute | solution.py:35
  54.3 0.7 constant_dynamic-update-slice_fusion.7
  55.0 0.8 constant_dynamic-update-slice_fusion.6
  55.9 0.8 constant_dynamic-update-slice_fusion.5
  56.7 0.8 constant_dynamic-update-slice_fusion.4
  57.5 0.7 constant_dynamic-update-slice_fusion.3
  58.3 0.7 constant_dynamic-update-slice_fusion.2
  59.0 6.0 %copy.115 = bf16[576,3072]{1,0:T(8,128)(2,1)} copy(bf16[576,3072]{0,1:T(8,128)(2,1)} %bitcast.30) | data formatting | bytes 7077888 | tf_op jit(solution)/shard_map/dot_general | solution.py:132
  65.0 4.7 %fusion.2 = f32[2,8,16,3,3,64]{5,2,4,3,0,1:T(8,128)S(1)} fusion(bf16[3,3,64,3072,1,1]{3,2,1,0,5,4:T(8,128)(2,1)} %bitcast.121, bf16[8,2,16,3072]{3,2,1,0:T(8,128)(2,1)} %all-gather.3.cloned.1.call-done), kind=kOutput, calls=%fused_computation.4 | convolution fusion | flops 905969664 | bytes 5701632 | tf_op jit(solution)/shard_map/dot_general | solution.py:132
  69.8 0.3 slice_reduce_fusion
  70.1 0.5 fusion.6
  71.3 1.4 broadcast_in_dim.7
  72.7 3.7 %all-to-all-start = ((bf16[16,128,384]{2,1,0:T(8,128)(2,1)}), bf16[16,128,384]{2,1,0:T(8,128)(2,1)S(1)}, u32[]{:S(2)}, u32[]{:S(2)}) async-start(bf16[16,128,384]{2,1,0:T(8,128)(2,1)} %bitcast.47), calls=%async_computation | async-start | bytes 3145728 | tf_op jit(solution)/shard_map/all_to_all | solution.py:152
  77.2 1.3 collective-permute-start.16
  78.5 17.4 %collective-permute-done.16 = bf16[128,256]{1,0:T(8,128)(2,1)S(1)} collective-permute-done((bf16[128,256]{1,0:T(8,128)(2,1)S(1)}, bf16[128,256]{1,0:T(8,128)(2,1)S(1)}, u32[]{:S(2)}, u32[]{:S(2)}) %collective-permute-start.16) | collective-permute-done | bytes 65568 | tf_op jit(solution)/shard_map/ppermute | solution.py:150
  95.9 1.3 all-to-all-done
  97.2 2.6 %shard_map.100 = bf16[256,192]{1,0:T(8,128)(2,1)S(1)} custom-call(bf16[256,256]{1,0:T(8,128)(2,1)S(1)} %pad_maximum_fusion.4.q_ref, bf16[2048,384]{1,0:T(8,128)(2,1)S(1)} %bitcast.117), custom_call_target="tpu_custom_call" | custom-call | flops 805306368 | bytes 1572864 | tf_op jit(solution)/shard_map/pallas_call | solution.py:65
  99.8 4.5 %collective-permute-start.17 = (bf16[128,192]{1,0:T(8,128)(2,1)S(1)}, bf16[128,192]{1,0:T(8,128)(2,1)S(1)}, u32[]{:S(2)}, u32[]{:S(2)}) collective-permute-start(bf16[128,192]{1,0:T(8,128)(2,1)S(1)} %get-tuple-element.19), channel_id=1, source_target_pairs={{0,128},{128,0},{1,129},{129,1},{2,130},{130,2},{3,131},{131,3},{4... | collective-permute-start | bytes 147464 | tf_op jit(solution)/shard_map/ppermute | solution.py:156
  104.3 1.7 %collective-permute-start.19 = (bf16[128,192]{1,0:T(8,128)(2,1)S(1)}, bf16[128,192]{1,0:T(8,128)(2,1)S(1)}, u32[]{:S(2)}, u32[]{:S(2)}) collective-permute-start(bf16[128,192]{1,0:T(8,128)(2,1)S(1)} %get-tuple-element.20), channel_id=1, source_target_pairs={{0,129},{1,128},{2,131},{3,130},{128,1},{129,0},{130,3},{131,2},{4... | collective-permute-start | bytes 147464 | tf_op jit(solution)/shard_map/ppermute | solution.py:158
  106.2 3.1 %collective-permute-done.18 = bf16[128,192]{1,0:T(8,128)(2,1)S(1)} collective-permute-done((bf16[128,192]{1,0:T(8,128)(2,1)S(1)}, bf16[128,192]{1,0:T(8,128)(2,1)S(1)}, u32[]{:S(2)}, u32[]{:S(2)}) %collective-permute-start.18) | collective-permute-done | bytes 49184 | tf_op jit(solution)/shard_map/ppermute | solution.py:157
  109.3 1.9 %collective-permute-done.19 = bf16[128,192]{1,0:T(8,128)(2,1)S(1)} collective-permute-done((bf16[128,192]{1,0:T(8,128)(2,1)S(1)}, bf16[128,192]{1,0:T(8,128)(2,1)S(1)}, u32[]{:S(2)}, u32[]{:S(2)}) %collective-permute-start.19) | collective-permute-done | bytes 49184 | tf_op jit(solution)/shard_map/ppermute | solution.py:158
  111.4 5.5 %all-gather.5.cloned.1.call-done = bf16[384,1536]{1,0:T(8,128)(2,1)} async-done(((bf16[24,1536]{1,0:T(8,128)(2,1)}), bf16[384,1536]{1,0:T(8,128)(2,1)}) %all-gather.5.cloned.1.call-update) | async-done | bytes 1179664 | tf_op jit(solution)/shard_map/all_gather | solution.py:100
  116.9 2.7 %convolution_convert_fusion = bf16[256,1536]{1,0:T(8,128)(2,1)} fusion(bf16[256,384]{1,0:T(8,128)(2,1)S(1)} %bitcast.128, bf16[384,1536]{1,0:T(8,128)(2,1)} %all-gather.5.cloned.1.call-done), kind=kOutput, calls=%fused_computation | convolution fusion | flops 302383104 | bytes 2162688 | tf_op jit(solution)/shard_map/dot_general | solution.py:172
  119.6 7.1 %all-to-all-start.1 = ((bf16[8,32,1536]{2,1,0:T(8,128)(2,1)}), bf16[8,32,1536]{2,1,0:T(8,128)(2,1)S(1)}, u32[]{:S(2)}, u32[]{:S(2)}) async-start(bf16[8,32,1536]{2,1,0:T(8,128)(2,1)} %bitcast.63), calls=%async_computation.1 | async-start | bytes 1572864 | tf_op jit(solution)/shard_map/all_to_all | solution.py:175
  127.4 2.0 %collective-permute-start = (s32[2]{0:T(128)S(1)}, s32[2]{0:T(128)S(1)}, u32[]{:S(2)}, u32[]{:S(2)}) collective-permute-start(s32[2]{0:T(128)S(1)} %pad_add_fusion), channel_id=1, source_target_pairs={{0,128},{128,0},{1,129},{129,1},{2,130},{130,2},{3,131},{131,3},{4... | collective-permute-start | bytes 32 | tf_op jit(solution)/shard_map/ppermute | solution.py:103
  129.5 0.8 collective-permute-done
  130.4 0.7 fusion.29
  138.6 0.7 fusion.28
  139.3 0.9 dynamic-slice_reduce_fusion.2
  140.2 8.5 %all-to-all-done.1 = bf16[8,32,1536]{2,1,0:T(8,128)(2,1)S(1)} async-done(((bf16[8,32,1536]{2,1,0:T(8,128)(2,1)}), bf16[8,32,1536]{2,1,0:T(8,128)(2,1)S(1)}, u32[]{:S(2)}, u32[]{:S(2)}) %all-to-all-start.1) | async-done | bytes 786464 | tf_op jit(solution)/shard_map/all_to_all | solution.py:175
  148.8 1.3 add_select_fusion.1
  150.1 2.1 %collective-permute-start.20 = (f32[16,1536]{1,0:T(8,128)S(1)}, f32[16,1536]{1,0:T(8,128)S(1)}, u32[]{:S(2)}, u32[]{:S(2)}) collective-permute-start(f32[16,1536]{1,0:T(8,128)S(1)} %get-tuple-element.18), channel_id=1, source_target_pairs={{0,128},{128,0},{1,129},{129,1},{2,130},{130,2},{3,131},{131,3},{4... | collective-permute-start | bytes 294920 | tf_op jit(solution)/shard_map/ppermute | solution.py:186
  152.3 0.9 collective-permute-done.20
  153.2 0.7 fusion.14
  (97 shorter events, 4.4 us)
Async XLA Ops:
  6.5 29.7 %copy-start = (bf16[24,3072]{1,0:T(8,128)(2,1)S(1)}, bf16[24,3072]{1,0:T(8,128)(2,1)}, u32[]{:S(2)}) copy-start(bf16[24,3072]{1,0:T(8,128)(2,1)} %param.13) | copy-start | bytes 442372
  6.5 11.9 %copy-start.1 = (bf16[192,3,384]{2,0,1:T(8,128)(2,1)S(1)}, bf16[192,3,384]{2,0,1:T(8,128)(2,1)}, u32[]{:S(2)}) copy-start(bf16[192,3,384]{2,0,1:T(8,128)(2,1)} %param.12) | copy-start | bytes 1327108
  6.5 58.4 %all-gather.3.cloned.1.call-start = ((), (), s32[]{:S(2)}) async-start(), calls=%async_computation.2 | async-start | bytes 1769472 | tf_op jit(solution)/shard_map/all_gather | solution.py:128
  12.5 24.4 %copy-start.4 = (f32[64]{0:T(128)S(1)}, f32[64]{0:T(128)}, u32[]{:S(2)}) copy-start(f32[64]{0:T(128)} %param.15) | copy-start | bytes 772
  13.4 4.3 %collective-permute-start.1 = (bf16[16,3072]{1,0:T(8,128)(2,1)S(1)}, bf16[16,3072]{1,0:T(8,128)(2,1)S(1)}, u32[]{:S(2)}, u32[]{:S(2)}) collective-permute-start(bf16[16,3072]{1,0:T(8,128)(2,1)S(1)} %constant_dynamic-update-slice_fusion), channel_id=1, source_target_pairs={{0,128},{128,0},{1,129},{129,1},{2,130},{130,2},{3,131},{131,3},{4... | collective-permute-start | bytes 294920 | tf_op jit(solution)/shard_map/ppermute | solution.py:124
  18.4 98.5 %all-gather.5.cloned.1.call-start = ((), (), s32[]{:S(2)}) async-start(), calls=%async_computation.3 | async-start | bytes 1253376 | tf_op jit(solution)/shard_map/all_gather | solution.py:100
  18.8 5.3 %collective-permute-start.2 = (bf16[96,576]{0,1:T(8,128)(2,1)S(1)}, bf16[96,576]{0,1:T(8,128)(2,1)S(1)}, u32[]{:S(2)}, u32[]{:S(2)}) collective-permute-start(bf16[96,576]{0,1:T(8,128)(2,1)S(1)} %bitcast.134), channel_id=1, source_target_pairs={{0,3},{1,0},{2,1},{3,2},{4,7},{5,4},{6,5},{7,6},{8,11},{9,8},{10,9... | collective-permute-start | bytes 331784 | tf_op jit(solution)/shard_map/ppermute | solution.py:24
  19.6 7.2 %collective-permute-start.3 = (bf16[96,576]{0,1:T(8,128)(2,1)S(1)}, bf16[96,576]{0,1:T(8,128)(2,1)S(1)}, u32[]{:S(2)}, u32[]{:S(2)}) collective-permute-start(bf16[96,576]{0,1:T(8,128)(2,1)S(1)} %bitcast.135), channel_id=1, source_target_pairs={{0,2},{1,3},{2,0},{3,1},{4,6},{5,7},{6,4},{7,5},{8,10},{9,11},{10,... | collective-permute-start | bytes 331784 | tf_op jit(solution)/shard_map/ppermute | solution.py:26
  20.2 9.9 %collective-permute-start.4 = (bf16[96,576]{0,1:T(8,128)(2,1)S(1)}, bf16[96,576]{0,1:T(8,128)(2,1)S(1)}, u32[]{:S(2)}, u32[]{:S(2)}) collective-permute-start(bf16[96,576]{0,1:T(8,128)(2,1)S(1)} %bitcast.136), channel_id=1, source_target_pairs={{0,1},{1,2},{2,3},{3,0},{4,5},{5,6},{6,7},{7,4},{8,9},{9,10},{10,1... | collective-permute-start | bytes 331784 | tf_op jit(solution)/shard_map/ppermute | solution.py:25
  20.9 12.4 %collective-permute-start.9 = (bf16[96,576]{0,1:T(8,128)(2,1)S(1)}, bf16[96,576]{0,1:T(8,128)(2,1)S(1)}, u32[]{:S(2)}, u32[]{:S(2)}) collective-permute-start(bf16[96,576]{0,1:T(8,128)(2,1)S(1)} %bitcast.130), channel_id=1, source_target_pairs={{0,12},{4,0},{8,4},{12,8},{1,13},{5,1},{9,5},{13,9},{2,14},{6,2},{... | collective-permute-start | bytes 331784 | tf_op jit(solution)/shard_map/ppermute | solution.py:24
  23.7 9.6 %collective-permute-start.10 = (bf16[96,576]{0,1:T(8,128)(2,1)S(1)}, bf16[96,576]{0,1:T(8,128)(2,1)S(1)}, u32[]{:S(2)}, u32[]{:S(2)}) collective-permute-start(bf16[96,576]{0,1:T(8,128)(2,1)S(1)} %bitcast.131), channel_id=1, source_target_pairs={{0,8},{4,12},{8,0},{12,4},{1,9},{5,13},{9,1},{13,5},{2,10},{6,14},... | collective-permute-start | bytes 331784 | tf_op jit(solution)/shard_map/ppermute | solution.py:26
  24.1 9.6 %collective-permute-start.11 = (bf16[96,576]{0,1:T(8,128)(2,1)S(1)}, bf16[96,576]{0,1:T(8,128)(2,1)S(1)}, u32[]{:S(2)}, u32[]{:S(2)}) collective-permute-start(bf16[96,576]{0,1:T(8,128)(2,1)S(1)} %bitcast.132), channel_id=1, source_target_pairs={{0,4},{4,8},{8,12},{12,0},{1,5},{5,9},{9,13},{13,1},{2,6},{6,10},{... | collective-permute-start | bytes 331784 | tf_op jit(solution)/shard_map/ppermute | solution.py:25
  30.5 12.9 %collective-permute-start.5 = (bf16[4,96,576]{2,1,0:T(8,128)(2,1)S(1)}, bf16[4,96,576]{2,1,0:T(8,128)(2,1)S(1)}, u32[]{:S(2)}, u32[]{:S(2)}) collective-permute-start(bf16[4,96,576]{2,1,0:T(8,128)(2,1)S(1)} %copy.105), channel_id=1, source_target_pairs={{0,12},{4,0},{8,4},{12,8},{1,13},{5,1},{9,5},{13,9},{2,14},{6,2},{... | collective-permute-start | bytes 1327112 | tf_op jit(solution)/shard_map/ppermute | solution.py:31
  33.3 13.6 %collective-permute-start.6 = (bf16[4,96,576]{2,1,0:T(8,128)(2,1)S(1)}, bf16[4,96,576]{2,1,0:T(8,128)(2,1)S(1)}, u32[]{:S(2)}, u32[]{:S(2)}) collective-permute-start(bf16[4,96,576]{2,1,0:T(8,128)(2,1)S(1)} %copy.105), channel_id=1, source_target_pairs={{0,4},{4,8},{8,12},{12,0},{1,5},{5,9},{9,13},{13,1},{2,6},{6,10},{... | collective-permute-start | bytes 1327112 | tf_op jit(solution)/shard_map/ppermute | solution.py:32
  34.1 13.2 %collective-permute-start.12 = (bf16[4,96,576]{2,1,0:T(8,128)(2,1)S(1)}, bf16[4,96,576]{2,1,0:T(8,128)(2,1)S(1)}, u32[]{:S(2)}, u32[]{:S(2)}) collective-permute-start(bf16[4,96,576]{2,1,0:T(8,128)(2,1)S(1)} %copy.112), channel_id=1, source_target_pairs={{0,3},{1,0},{2,1},{3,2},{4,7},{5,4},{6,5},{7,6},{8,11},{9,8},{10,9... | collective-permute-start | bytes 1327112 | tf_op jit(solution)/shard_map/ppermute | solution.py:31
  36.3 12.7 %collective-permute-start.13 = (bf16[4,96,576]{2,1,0:T(8,128)(2,1)S(1)}, bf16[4,96,576]{2,1,0:T(8,128)(2,1)S(1)}, u32[]{:S(2)}, u32[]{:S(2)}) collective-permute-start(bf16[4,96,576]{2,1,0:T(8,128)(2,1)S(1)} %copy.112), channel_id=1, source_target_pairs={{0,1},{1,2},{2,3},{3,0},{4,5},{5,6},{6,7},{7,4},{8,9},{9,10},{10,1... | collective-permute-start | bytes 1327112 | tf_op jit(solution)/shard_map/ppermute | solution.py:32
  43.4 7.4 %collective-permute-start.7 = (bf16[2,96,576]{2,1,0:T(8,128)(2,1)S(1)}, bf16[2,96,576]{2,1,0:T(8,128)(2,1)S(1)}, u32[]{:S(2)}, u32[]{:S(2)}) collective-permute-start(bf16[2,96,576]{2,1,0:T(8,128)(2,1)S(1)} %slice.155), channel_id=1, source_target_pairs={{0,12},{4,0},{8,4},{12,8},{1,13},{5,1},{9,5},{13,9},{2,14},{6,2},{... | collective-permute-start | bytes 663560 | tf_op jit(solution)/shard_map/ppermute | solution.py:34
  47.0 7.3 %collective-permute-start.8 = (bf16[2,96,576]{2,1,0:T(8,128)(2,1)S(1)}, bf16[2,96,576]{2,1,0:T(8,128)(2,1)S(1)}, u32[]{:S(2)}, u32[]{:S(2)}) collective-permute-start(bf16[2,96,576]{2,1,0:T(8,128)(2,1)S(1)} %slice.156), channel_id=1, source_target_pairs={{0,4},{4,8},{8,12},{12,0},{1,5},{5,9},{9,13},{13,1},{2,6},{6,10},{... | collective-permute-start | bytes 663560 | tf_op jit(solution)/shard_map/ppermute | solution.py:35
  47.3 10.3 %collective-permute-start.14 = (bf16[2,96,576]{2,1,0:T(8,128)(2,1)S(1)}, bf16[2,96,576]{2,1,0:T(8,128)(2,1)S(1)}, u32[]{:S(2)}, u32[]{:S(2)}) collective-permute-start(bf16[2,96,576]{2,1,0:T(8,128)(2,1)S(1)} %slice.157), channel_id=1, source_target_pairs={{0,3},{1,0},{2,1},{3,2},{4,7},{5,4},{6,5},{7,6},{8,11},{9,8},{10,9... | collective-permute-start | bytes 663560 | tf_op jit(solution)/shard_map/ppermute | solution.py:34
  49.0 9.3 %collective-permute-start.15 = (bf16[2,96,576]{2,1,0:T(8,128)(2,1)S(1)}, bf16[2,96,576]{2,1,0:T(8,128)(2,1)S(1)}, u32[]{:S(2)}, u32[]{:S(2)}) collective-permute-start(bf16[2,96,576]{2,1,0:T(8,128)(2,1)S(1)} %slice.158), channel_id=1, source_target_pairs={{0,1},{1,2},{2,3},{3,0},{4,5},{5,6},{6,7},{7,4},{8,9},{9,10},{10,1... | collective-permute-start | bytes 663560 | tf_op jit(solution)/shard_map/ppermute | solution.py:35
  70.6 5.8 %copy-start.5 = (f32[64]{0:T(128)S(1)}, f32[64]{0:T(128)}, u32[]{:S(2)}) copy-start(f32[64]{0:T(128)} %param.14) | copy-start | bytes 772
  72.7 24.6 %all-to-all-start = ((bf16[16,128,384]{2,1,0:T(8,128)(2,1)}), bf16[16,128,384]{2,1,0:T(8,128)(2,1)S(1)}, u32[]{:S(2)}, u32[]{:S(2)}) async-start(bf16[16,128,384]{2,1,0:T(8,128)(2,1)} %bitcast.47), calls=%async_computation | async-start | bytes 3145728 | tf_op jit(solution)/shard_map/all_to_all | solution.py:152
  77.2 18.7 %collective-permute-start.16 = (bf16[128,256]{1,0:T(8,128)(2,1)S(1)}, bf16[128,256]{1,0:T(8,128)(2,1)S(1)}, u32[]{:S(2)}, u32[]{:S(2)}) collective-permute-start(bf16[128,256]{1,0:T(8,128)(2,1)S(1)} %get-tuple-element.22), channel_id=1, source_target_pairs={{0,1},{1,0},{2,3},{3,2},{4,5},{5,4},{6,7},{7,6},{8,9},{9,8},{10,11... | collective-permute-start | bytes 196616 | tf_op jit(solution)/shard_map/ppermute | solution.py:150
  97.2 41.4 %copy-start.3 = (f32[50]{0:T(128)S(1)}, f32[50]{0:T(128)}, u32[]{:S(2)}) copy-start(f32[50]{0:T(128)} %param.18) | copy-start | bytes 604
  97.2 56.0 %copy-start.2 = (f32[16,3072]{1,0:T(8,128)S(1)}, f32[16,3072]{1,0:T(8,128)}, u32[]{:S(2)}) copy-start(f32[16,3072]{1,0:T(8,128)} %param.11) | copy-start | bytes 589828
  99.8 6.2 %collective-permute-start.17 = (bf16[128,192]{1,0:T(8,128)(2,1)S(1)}, bf16[128,192]{1,0:T(8,128)(2,1)S(1)}, u32[]{:S(2)}, u32[]{:S(2)}) collective-permute-start(bf16[128,192]{1,0:T(8,128)(2,1)S(1)} %get-tuple-element.19), channel_id=1, source_target_pairs={{0,128},{128,0},{1,129},{129,1},{2,130},{130,2},{3,131},{131,3},{4... | collective-permute-start | bytes 147464 | tf_op jit(solution)/shard_map/ppermute | solution.py:156
  104.3 5.0 %collective-permute-start.18 = (bf16[128,192]{1,0:T(8,128)(2,1)S(1)}, bf16[128,192]{1,0:T(8,128)(2,1)S(1)}, u32[]{:S(2)}, u32[]{:S(2)}) collective-permute-start(bf16[128,192]{1,0:T(8,128)(2,1)S(1)} %get-tuple-element.20), channel_id=1, source_target_pairs={{0,1},{1,0},{2,3},{3,2},{4,5},{5,4},{6,7},{7,6},{8,9},{9,8},{10,11... | collective-permute-start | bytes 147464 | tf_op jit(solution)/shard_map/ppermute | solution.py:157
  104.3 6.9 %collective-permute-start.19 = (bf16[128,192]{1,0:T(8,128)(2,1)S(1)}, bf16[128,192]{1,0:T(8,128)(2,1)S(1)}, u32[]{:S(2)}, u32[]{:S(2)}) collective-permute-start(bf16[128,192]{1,0:T(8,128)(2,1)S(1)} %get-tuple-element.20), channel_id=1, source_target_pairs={{0,129},{1,128},{2,131},{3,130},{128,1},{129,0},{130,3},{131,2},{4... | collective-permute-start | bytes 147464 | tf_op jit(solution)/shard_map/ppermute | solution.py:158
  119.6 29.1 %all-to-all-start.1 = ((bf16[8,32,1536]{2,1,0:T(8,128)(2,1)}), bf16[8,32,1536]{2,1,0:T(8,128)(2,1)S(1)}, u32[]{:S(2)}, u32[]{:S(2)}) async-start(bf16[8,32,1536]{2,1,0:T(8,128)(2,1)} %bitcast.63), calls=%async_computation.1 | async-start | bytes 1572864 | tf_op jit(solution)/shard_map/all_to_all | solution.py:175
  127.4 2.9 %collective-permute-start = (s32[2]{0:T(128)S(1)}, s32[2]{0:T(128)S(1)}, u32[]{:S(2)}, u32[]{:S(2)}) collective-permute-start(s32[2]{0:T(128)S(1)} %pad_add_fusion), channel_id=1, source_target_pairs={{0,128},{128,0},{1,129},{129,1},{2,130},{130,2},{3,131},{131,3},{4... | collective-permute-start | bytes 32 | tf_op jit(solution)/shard_map/ppermute | solution.py:103
  150.1 3.1 %collective-permute-start.20 = (f32[16,1536]{1,0:T(8,128)S(1)}, f32[16,1536]{1,0:T(8,128)S(1)}, u32[]{:S(2)}, u32[]{:S(2)}) collective-permute-start(f32[16,1536]{1,0:T(8,128)S(1)} %get-tuple-element.18), channel_id=1, source_target_pairs={{0,128},{128,0},{1,129},{129,1},{2,130},{130,2},{3,131},{131,3},{4... | collective-permute-start | bytes 294920 | tf_op jit(solution)/shard_map/ppermute | solution.py:186
Sparse Core Ops, SparseCore 0:
  18.5 37.1 all-gather.2
  58.1 58.7 all-gather.4

commit v2 on v1

v2 whole, which is shorter than its diff:
```python
import jax
import jax.numpy as jnp
from jax import lax
from jax.experimental import pallas as pl
from jax.experimental.pallas import tpu as pltpu
from jax.sharding import Mesh, PartitionSpec as P

HD = 64
BF = jnp.bfloat16
F32 = jnp.float32
SMALL = ("c", "y0", "x0")
PLANE = ("y1", "y0", "x1", "x0")
VMEM = pl.BlockSpec(memory_space=pltpu.VMEM)
SMEM = pl.BlockSpec(memory_space=pltpu.SMEM)
SWAP = [(0, 1), (1, 0)]


def plane_pairs(dy, dx):
    return [
        (y * 4 + x, (y - dy) % 4 * 4 + (x - dx) % 4) for y in range(4) for x in range(4)
    ]


def small_pairs(target):
    pairs = []
    for core in range(2):
        for y in range(2):
            for x in range(2):
                to_core, to_y, to_x = target(core, y, x)
                pairs.append((core * 4 + y * 2 + x, to_core * 4 + to_y * 2 + to_x))
    return pairs


def ring_of_four(block, dy, dx):
    after = lax.ppermute(block, PLANE, plane_pairs(dy, dx))
    before = lax.ppermute(block, PLANE, plane_pairs(-dy, -dx))
    across = lax.ppermute(block, PLANE, plane_pairs(2 * dy, 2 * dx))
    return jnp.stack([block, after, across, before])


def ring_forwarded(block, dy, dx):
    after = lax.ppermute(block, PLANE, plane_pairs(dy, dx))
    before = lax.ppermute(block, PLANE, plane_pairs(-dy, -dx))
    low = lax.ppermute(after[:2], PLANE, plane_pairs(dy, dx))
    high = lax.ppermute(before[2:], PLANE, plane_pairs(-dy, -dx))
    return [block, after, before, low, high]


def low_lanes():
    return lax.broadcasted_iota(jnp.int32, (1, 128), 1) < 64


def roll64(tile):
    return pltpu.roll(tile, 64, 1)


def normalize_pair(tile, gains, low):
    def per_head(values):
        first = jnp.sum(jnp.where(low, values, 0.0), axis=1, keepdims=True)
        second = jnp.sum(jnp.where(low, 0.0, values), axis=1, keepdims=True)
        return jnp.where(low, first, second) * (1.0 / HD)

    centered = tile - per_head(tile)
    return centered * lax.rsqrt(per_head(centered * centered) + 1e-06) * gains


def project_kernel(
    core_ref, own_ref, other_ref, gain_ref, *refs
):
    pieces, (kv_ref, q_ref), acc = refs[:10], refs[10:12], refs[12]
    low = low_lanes()
    first_core = core_ref[0] == 0

    def term(i):
        if i % 4 == 3:
            low_half, high_half = pieces[i // 4 * 5 + 3], pieces[i // 4 * 5 + 4]
            block = jnp.concatenate([low_half[...], high_half[...]], axis=0)
        else:
            block = pieces[i // 4 * 5 + i % 4][...]
        columns = pl.ds(i * 384, 384)
        for r, ref in enumerate((own_ref, other_ref)):
            value = jnp.dot(ref[:, columns], block, preferred_element_type=F32)
            if i == 0:
                acc[r] = value
            else:
                acc[r] += value

    for i in range(8):
        term(i)

    def of_step(step, columns):
        own, other = acc[0, :, columns], acc[1, :, columns]
        return jnp.where(first_core, own, other) if step == 0 else jnp.where(first_core, other, own)

    q_gain, k_gain = gain_ref[0:1, :], gain_ref[1:2, :]
    for step in range(2):
        tiles = []
        for t in range(3):
            raw = of_step(step, slice(t * 128, t * 128 + 128))
            normed = normalize_pair(raw, k_gain, low)
            tiles.append(jnp.where(first_core, normed, raw))
        lo, hi = slice(0, 64), slice(64, 128)
        for half, (t, m) in enumerate(
            (
                (tiles[0], jnp.where(low, tiles[1][lo], roll64(tiles[1][hi]))),
                (tiles[2], jnp.where(low, roll64(tiles[1][lo]), tiles[1][hi])),
            )
        ):
            kv_ref[half, step, :, 0:128] = t[lo].astype(BF)
            kv_ref[half, step, :, 128:256] = t[hi].astype(BF)
            kv_ref[half, step, :, 256:384] = m.astype(BF)
        pair = normalize_pair(of_step(step, slice(384, 512)), q_gain, low).astype(BF)
        last = of_step(step, slice(512, 576))
        last = jnp.concatenate([last, last], axis=1)
        last = normalize_pair(last, q_gain, low).astype(BF)
        factor = jnp.asarray(HD**-0.5, BF)
        q_ref[step, :, 0:128] = pair[lo] * factor
        q_ref[step, :, 128:256] = pair[hi] * factor
        q_ref[step, :, 256:384] = jnp.where(low, last[lo], last[hi]) * factor


def project(core, own, other, gains, pieces):
    rows = own.shape[0]
    return pl.pallas_call(
        project_kernel,
        out_shape=(
            jax.ShapeDtypeStruct((2, 2, 64, 384), BF),
            jax.ShapeDtypeStruct((2, 64, 384), BF),
        ),
        in_specs=[SMEM] + [VMEM] * 13,
        out_specs=(VMEM, VMEM),
        scratch_shapes=[pltpu.VMEM((2, rows, 576), F32)],
        compiler_params=pltpu.CompilerParams(vmem_limit_bytes=40 * 1024 * 1024),
        cost_estimate=pl.CostEstimate(
            flops=4 * rows * 3072 * 576, bytes_accessed=3072 * 576 * 2, transcendentals=0
        ),
    )(core, own, other, gains, *pieces)


def attention_kernel(core_ref, q0_ref, q1_ref, mine_ref, theirs_ref, o0_ref, o1_ref):
    low = low_lanes()
    first_core = core_ref[0] == 0
    dims = (((1,), (1,)), ((), ()))

    def key(t):
        a, b = mine_ref[:, t * 128 : t * 128 + 128], theirs_ref[:, t * 128 : t * 128 + 128]
        return jnp.where(first_core, a, b)

    def value(t):
        a, b = mine_ref[:, t * 128 : t * 128 + 128], theirs_ref[:, t * 128 : t * 128 + 128]
        return jnp.where(first_core, b, a)

    def head(q_a, q_b, k_a, k_b, v_a, v_b, shifted):
        s_a = lax.dot_general(q_a, k_a, dims, preferred_element_type=F32)
        s_b = lax.dot_general(q_b, k_b, dims, preferred_element_type=F32)
        peak = jnp.maximum(
            jnp.max(s_a, axis=-1, keepdims=True), jnp.max(s_b, axis=-1, keepdims=True)
        )
        w_a, w_b = jnp.exp(s_a - peak), jnp.exp(s_b - peak)
        total = jnp.sum(w_a, axis=-1, keepdims=True) + jnp.sum(w_b, axis=-1, keepdims=True)
        m_a = jnp.dot(w_a.astype(BF), v_a, preferred_element_type=F32)
        m_b = jnp.dot(w_b.astype(BF), v_b, preferred_element_type=F32)
        return (m_a + (roll64(m_b) if shifted else m_b)) / total

    q_pair = jnp.concatenate(
        [q0_ref[:, 0:128], q1_ref[:, 0:128], q0_ref[:, 128:256], q1_ref[:, 128:256]], axis=0
    )
    zero = jnp.zeros_like(q_pair)
    q_first, q_second = jnp.where(low, q_pair, zero), jnp.where(low, zero, q_pair)
    k_lo, k_hi, v_lo, v_hi = key(0), key(1), value(0), value(1)
    first = head(q_first, q_first, k_lo, k_hi, v_lo, v_hi, False)
    second = head(q_second, q_second, k_lo, k_hi, v_lo, v_hi, False)
    both = jnp.where(low, first, second).astype(BF)
    last = jnp.concatenate([q0_ref[:, 256:384], q1_ref[:, 256:384]], axis=0).astype(F32)
    turned = roll64(last)
    q_low = jnp.where(low, jnp.concatenate([last, turned], axis=0), 0.0).astype(BF)
    q_high = jnp.where(low, 0.0, jnp.concatenate([turned, last], axis=0)).astype(BF)
    third = head(q_low, q_high, key(2), key(2), value(2), value(2), True)
    for i, ref in enumerate((o0_ref, o1_ref)):
        lo, hi = slice(64 * i, 64 * i + 64), slice(128 + 64 * i, 192 + 64 * i)
        ref[:, 0:128] = both[lo]
        ref[:, 128:256] = both[hi]
        ref[:, 256:384] = jnp.where(low, third[lo], roll64(third[hi])).astype(BF)


def attention(core, q0, q1, mine, theirs):
    keys = 2 * mine.shape[0]
    return pl.pallas_call(
        attention_kernel,
        out_shape=(jax.ShapeDtypeStruct((64, 384), BF),) * 2,
        in_specs=[SMEM] + [VMEM] * 4,
        out_specs=(VMEM, VMEM),
        compiler_params=pltpu.CompilerParams(vmem_limit_bytes=40 * 1024 * 1024),
        cost_estimate=pl.CostEstimate(
            flops=4 * 256 * keys * 3 * 128,
            bytes_accessed=mine.size * 4,
            transcendentals=256 * keys * 3,
        ),
    )(core, q0, q1, mine, theirs)


def output_kernel(bits_ref, p00_ref, p01_ref, p10_ref, p11_ref, w_ref, o_ref):
    low = low_lanes()
    first_core, first_step = bits_ref[0] == 0, bits_ref[1] == 0

    def half_of(step, half, t):
        columns = slice(t * 128, t * 128 + 128)

        def of(near, far):
            a, b = near[:, columns].astype(F32), far[:, columns].astype(F32)
            return jnp.where(first_core, a, b) if half == 0 else jnp.where(first_core, b, a)

        this, that = of(p00_ref, p01_ref), of(p10_ref, p11_ref)
        return jnp.where(first_step, this, that) if step == 0 else jnp.where(first_step, that, this)

    rows = []
    for step in range(2):
        near = [half_of(step, 0, t) for t in range(3)]
        far = [half_of(step, 1, t) for t in range(3)]
        for part in range(2):
            if part == 0:
                middle = jnp.where(low, near[2], roll64(far[2]))
            else:
                middle = jnp.where(low, roll64(near[2]), far[2])
            rows.append(jnp.concatenate([near[part], middle, far[part]], axis=1).astype(BF))
    features = jnp.concatenate(rows, axis=0)
    for column in range(0, w_ref.shape[1], 512):
        columns = slice(column, column + 512)
        result = jnp.dot(features, w_ref[:, columns], preferred_element_type=F32).astype(BF)
        for step in range(2):
            for z in range(8):
                at = step * 128 + z * 16
                o_ref[z, step * 16 : step * 16 + 16, columns] = result[at : at + 16]


def output_projection(bits, parts, w_rows):
    width = w_rows.shape[1]
    return pl.pallas_call(
        output_kernel,
        out_shape=jax.ShapeDtypeStruct((8, 32, width), BF),
        in_specs=[SMEM] + [VMEM] * 5,
        out_specs=VMEM,
        compiler_params=pltpu.CompilerParams(vmem_limit_bytes=40 * 1024 * 1024),
        cost_estimate=pl.CostEstimate(
            flops=2 * 256 * 384 * width, bytes_accessed=w_rows.size * 2, transcendentals=0
        ),
    )(bits, *parts, w_rows)


def on_device(
    states, start, w_qkv, w_out, q_gain, k_gain, mod_table, step_index, coef_table, coef_index
):
    width = states.shape[2]
    tokens = states.shape[1]
    half = width // 2
    core = lax.axis_index("c")
    at_y = lax.axis_index(("y1", "y0"))
    at_x = lax.axis_index(("x1", "x0"))
    first_core = core == 0
    core_bit = core.astype(jnp.int32).reshape(1)
    bits = jnp.stack([core, lax.axis_index("x0")]).astype(jnp.int32)

    row = lax.dynamic_index_in_dim(mod_table, step_index[0], 0, True)
    current = states[0]
    middle = jnp.mean(current, axis=-1, keepdims=True)
    spread = jnp.mean((current - middle) ** 2, axis=-1, keepdims=True)
    normed = (
        (current - middle) * lax.rsqrt(spread + 1e-05) * (1.0 + row[:, width : 2 * width])
        + row[:, :width]
    ).astype(BF)
    blocks = normed.reshape(tokens, 4, 4, 192)
    blocks = lax.dynamic_slice_in_dim(jnp.concatenate([blocks, blocks], axis=1), at_y, 4, axis=1)
    blocks = lax.dynamic_slice_in_dim(jnp.concatenate([blocks, blocks], axis=2), at_x, 4, axis=2)
    order = [0, 1, 3, 2]
    part_x = jnp.concatenate([blocks[:, i : i + 1, :, :96] for i in order], axis=1)
    part_y = jnp.concatenate([blocks[:, :, i : i + 1, 96:] for i in order], axis=2)
    arranged = jnp.concatenate(
        [part_x.reshape(tokens, half), jnp.swapaxes(part_y, 1, 2).reshape(tokens, half)], axis=1
    )
    own = lax.all_to_all(
        jnp.broadcast_to(arranged[None], (8, tokens, width)), "z", 0, 0, tiled=True
    ).reshape(8 * tokens, width)
    other = lax.ppermute(own, "c", SWAP)

    w_kv = jnp.where(first_core, w_qkv[:, 1], w_qkv[:, 2])
    w_q = w_qkv[:, 0]
    w_q = jnp.where(
        first_core, w_q[:, :192], jnp.concatenate([w_q[:, 256:], w_q[:, 192:256]], axis=1)
    )
    w_core = jnp.concatenate([w_kv, w_q], axis=1)
    by_x = ring_of_four(w_core[:96], 0, 1)
    by_y = ring_of_four(w_core[96:], 1, 0)
    pieces = ring_forwarded(by_x, 1, 0) + ring_forwarded(by_y, 0, 1)
    pieces = [p.reshape(-1, 576) for p in pieces]

    gains = jnp.stack([jnp.tile(q_gain, 2), jnp.tile(k_gain, 2)])
    keys_values, queries = project(core_bit, own, other, gains, pieces)

    outgoing = jnp.broadcast_to(keys_values[None, :, None], (2, 2, 2, 2, 64, 384))
    mine = lax.all_to_all(outgoing.reshape(16, 64, 384), PLANE, 0, 0, tiled=True)
    mine = mine.reshape(1024, 384)
    theirs = lax.ppermute(mine, "c", SWAP)
    first_x = lax.axis_index("x0") == 0
    this_q = jnp.where(first_x, queries[0], queries[1])
    that_q = jnp.where(first_x, queries[1], queries[0])
    q0 = lax.ppermute(this_q, SMALL, small_pairs(lambda c, y, x: (y, c, x)))
    q1 = lax.ppermute(that_q, SMALL, small_pairs(lambda c, y, x: (y, c, 1 - x)))

    w_half = lax.dynamic_slice_in_dim(w_out, core * half, half, axis=1)
    w_half, mine = lax.optimization_barrier((w_half, mine))
    w_rows = lax.all_to_all(
        jnp.broadcast_to(w_half[None], (16,) + w_half.shape), PLANE, 0, 0, tiled=True
    ).reshape(384, half)

    o0, o1 = attention(core_bit, q0, q1, mine, theirs)

    parts = [
        lax.ppermute(o, SMALL, small_pairs(lambda c, y, x, k=k, m=m: (y ^ m, c, x ^ k)))
        for k, o in enumerate((o0, o1))
        for m in range(2)
    ]
    share = output_projection(bits, parts, w_rows)
    arrived = lax.all_to_all(share, "z", 0, 0, tiled=True)
    mixed = jnp.sum(arrived.astype(F32), axis=0).reshape(2, tokens, half)

    own_index = jnp.concatenate([step_index, coef_index])
    other_index = lax.ppermute(own_index, "c", SWAP)

    def weighted(index, drift):
        gate = lax.dynamic_slice(mod_table, (index[0], 2 * width + core * half), (1, half))
        return coef_table[index[1]] * (gate * drift)

    first = weighted(jnp.where(first_core, own_index, other_index), mixed[0])
    second = first + weighted(jnp.where(first_core, other_index, own_index), mixed[1])
    kept = jnp.where(first_core, first, second)
    given = jnp.where(first_core, second, first)
    got = lax.ppermute(given, "c", SWAP)
    moved = jnp.where(
        first_core,
        jnp.concatenate([kept, got], axis=1),
        jnp.concatenate([got, kept], axis=1),
    )
    return (start + moved)[None]


def solution(mesh):
    grid = Mesh(mesh.devices.reshape(2, 8, 2, 2, 2, 2), ("c", "z") + PLANE)
    tokens = ("z",) + PLANE
    in_specs = (
        P("c", tokens, None),
        P(tokens, None),
        P(PLANE, None, "z"),
        P(tokens, None),
        P(),
        P(),
        P(),
        P("c"),
        P(),
        P("c"),
    )
    return jax.shard_map(
        on_device, mesh=grid, in_specs=in_specs, out_specs=P("c", tokens, None), check_vma=False
    )
```

time: 161 us -> 157 us (0.975)
  between operations: 22.9 us -> 9.23 us
  waiting for transfers between devices: 52.4 us -> 65 us
  local copies, waits for them, and re-layouts: 22.4 us -> 12.1 us
  starting transfers between devices: 44.3 us -> 54.3 us
  matrix products: 7.41 us -> 0 us
  Pallas kernels: 2.57 us -> 9.12 us
  other arithmetic: 8.79 us -> 6.8 us
    all_to_all x2 -> x4, waiting for transfers between devices: 9.83 us -> 32.4 us  [the longest x1 12.3 us: on_device(): lax.all_to_all(outgoing.reshape(16, 64, 384), PLANE, 0, 0, tiled=True)]
    all_to_all x2 -> x4, starting transfers between devices: 10.8 us -> 20.3 us  [the longest x1 9.01 us: on_device(): lax.all_to_all(jnp.broadcast_to(arranged[None], (8, tokens, width)), 'z',...]
    dot_general x2 -> x0, matrix products: 7.41 us -> none  [the longest x1 4.68 us: on_device(): jnp.dot(gathered.reshape(2 * rows, width), weights, preferred_element_typ...]
    pallas_call x1 -> x3, Pallas kernels: 2.57 us -> 9.12 us  [the longest x1 4.2 us: project(): pl.pallas_call(project_kernel, out_shape=(jax.ShapeDtypeStruct((2, 2, 64,...]
    dot_general x1 -> x0, local copies, waits for them, and re-layouts: 5.96 us -> none  [on_device(): jnp.dot(gathered.reshape(2 * rows, width), weights, preferred_element_typ...]
    all_gather x2 -> x0, waiting for transfers between devices: 5.51 us -> none  [the longest x1 5.51 us: on_device(): w_out_rows = lax.all_gather(w_out_half, ('y', 'x'), axis=0, tiled=True)]
    unnamed x22 -> x16, local copies, waits for them, and re-layouts: 7.23 us -> 1.89 us
    ppermute x21 -> x24, waiting for transfers between devices: 37 us -> 32.6 us  [the longest x1 8.7 us: on_device(): q0 = lax.ppermute(this_q, SMALL, small_pairs(lambda c, y, x: (y, c, x)))]
  transfers between devices with their start and end apart: 25 -> 28, of which waited for: 14 -> 15; matrix products, arithmetic and copies ran while one was open for 17% -> 4% of each run, Pallas kernels for 2% -> 2%
where the time goes in v2:
time: 157 us
  waiting for transfers between devices  65 us (41%)
  starting transfers between devices  54.3 us (35%)
  local copies, waits for them, and re-layouts  12.1 us (8%)
  between operations  9.23 us (6%)
  Pallas kernels  9.12 us (6%)
  other arithmetic  6.8 us (4%)
    all_to_all x1, waiting for transfers between devices, on_device(): lax.all_to_all(outgoing.reshape(16, 64, 384), PLANE, 0, 0, tiled=True)  12.3 us
    all_to_all x1, waiting for transfers between devices, on_device(): arrived = lax.all_to_all(share, 'z', 0, 0, tiled=True)  11.1 us
    all_to_all x1, waiting for transfers between devices, on_device(): lax.all_to_all(jnp.broadcast_to(arranged[None], (8, tokens, width)), 'z',...  9.02 us
    all_to_all x1, starting transfers between devices, on_device(): lax.all_to_all(jnp.broadcast_to(arranged[None], (8, tokens, width)), 'z',...  9.01 us
    ppermute x1, waiting for transfers between devices, on_device(): q0 = lax.ppermute(this_q, SMALL, small_pairs(lambda c, y, x: (y, c, x)))  8.7 us
    ppermute x2, waiting for transfers between devices, ring_forwarded(): after = lax.ppermute(block, PLANE, plane_pairs(dy, dx))  6.71 us
    ppermute x2, starting transfers between devices, ring_forwarded(): low = lax.ppermute(after[:2], PLANE, plane_pairs(dy, dx))  6 us
    ppermute x2, starting transfers between devices, ring_forwarded(): after = lax.ppermute(block, PLANE, plane_pairs(dy, dx))  5.37 us
  transfers between devices with their start and end apart: 28, of which 15 were waited for; matrix products, arithmetic and copies ran while one was open for 4% of the time, Pallas kernels for 2%

profile of v2, /device:TPU:1, one launch (start us, length us, event | category | flops | bytes accessed | tf_op | source)
XLA Modules:
  0.0 156.6 jit_solution(17478409879769647406)
XLA Ops:
  0.7 1.1 fusion.13
  1.9 1.1 squeeze.40
  3.1 1.1 reduce_sum.27
  4.2 1.1 fusion.7
  5.3 0.2 fusion.3
  5.5 0.3 fusion.9
  5.8 0.2 fusion.8
  6.3 0.1 pad_maximum_fusion.4
  6.5 0.1 reshape.99
  6.8 1.0 broadcast_in_dim.8
  7.8 9.0 %all-to-all-start = ((bf16[8,16,3072]{2,1,0:T(8,128)(2,1)}), bf16[8,16,3072]{2,1,0:T(8,128)(2,1)S(1)}, u32[]{:S(2)}, u32[]{:S(2)}) async-start(bf16[8,16,3072]{2,1,0:T(8,128)(2,1)} %broadcast_in_dim.8), calls=%async_computation | async-start | bytes 1572864 | tf_op jit(solution)/shard_map/all_to_all | solution.py:280
  17.0 2.8 %collective-permute-start.9 = (bf16[96,576]{1,0:T(8,128)(2,1)S(1)}, bf16[96,576]{1,0:T(8,128)(2,1)S(1)}, u32[]{:S(2)}, u32[]{:S(2)}) collective-permute-start(bf16[96,576]{1,0:T(8,128)(2,1)S(1)} %get-tuple-element.23), channel_id=1, source_target_pairs={{0,12},{1,13},{2,14},{3,15},{4,0},{5,1},{6,2},{7,3},{8,4},{9,5},{1... | collective-permute-start | bytes 331784 | tf_op jit(solution)/shard_map/ppermute | solution.py:35
  19.9 0.3 collective-permute-start.10
  20.2 0.7 collective-permute-start.11
  20.9 2.5 %collective-permute-start.2 = (bf16[96,576]{1,0:T(8,128)(2,1)S(1)}, bf16[96,576]{1,0:T(8,128)(2,1)S(1)}, u32[]{:S(2)}, u32[]{:S(2)}) collective-permute-start(bf16[96,576]{1,0:T(8,128)(2,1)S(1)} %get-tuple-element.24), channel_id=1, source_target_pairs={{0,3},{1,0},{2,1},{3,2},{4,7},{5,4},{6,5},{7,6},{8,11},{9,8},{10,9... | collective-permute-start | bytes 331784 | tf_op jit(solution)/shard_map/ppermute | solution.py:35
  23.4 0.5 collective-permute-start.3
  23.9 0.6 collective-permute-start.4
  24.5 0.9 collective-permute-done.10
  25.4 3.3 %collective-permute-done.11 = bf16[96,576]{1,0:T(8,128)(2,1)S(1)} collective-permute-done((bf16[96,576]{1,0:T(8,128)(2,1)S(1)}, bf16[96,576]{1,0:T(8,128)(2,1)S(1)}, u32[]{:S(2)}, u32[]{:S(2)}) %collective-permute-start.11) | collective-permute-done | bytes 110624 | tf_op jit(solution)/shard_map/ppermute | solution.py:36
  28.8 2.6 %collective-permute-start.12 = (bf16[4,96,576]{2,1,0:T(8,128)(2,1)S(1)}, bf16[4,96,576]{2,1,0:T(8,128)(2,1)S(1)}, u32[]{:S(2)}, u32[]{:S(2)}) collective-permute-start(bf16[4,96,576]{2,1,0:T(8,128)(2,1)S(1)} %pad_maximum_fusion.1), channel_id=1, source_target_pairs={{0,3},{1,0},{2,1},{3,2},{4,7},{5,4},{6,5},{7,6},{8,11},{9,8},{10,9... | collective-permute-start | bytes 1327112 | tf_op jit(solution)/shard_map/ppermute | solution.py:42
  31.3 9.0 %all-to-all-done = bf16[8,16,3072]{2,1,0:T(8,128)(2,1)S(1)} async-done(((bf16[8,16,3072]{2,1,0:T(8,128)(2,1)}), bf16[8,16,3072]{2,1,0:T(8,128)(2,1)S(1)}, u32[]{:S(2)}, u32[]{:S(2)}) %all-to-all-start) | async-done | bytes 786464 | tf_op jit(solution)/shard_map/all_to_all | solution.py:280
  40.4 0.5 collective-permute-start.1
  41.0 2.8 %collective-permute-start.5 = (bf16[4,96,576]{2,1,0:T(8,128)(2,1)S(1)}, bf16[4,96,576]{2,1,0:T(8,128)(2,1)S(1)}, u32[]{:S(2)}, u32[]{:S(2)}) collective-permute-start(bf16[4,96,576]{2,1,0:T(8,128)(2,1)S(1)} %pad_maximum_fusion), channel_id=1, source_target_pairs={{0,12},{1,13},{2,14},{3,15},{4,0},{5,1},{6,2},{7,3},{8,4},{9,5},{1... | collective-permute-start | bytes 1327112 | tf_op jit(solution)/shard_map/ppermute | solution.py:42
  43.8 0.7 slice.133
  44.5 2.5 %collective-permute-start.14 = (bf16[2,96,576]{2,1,0:T(8,128)(2,1)}, bf16[2,96,576]{2,1,0:T(8,128)(2,1)}, u32[]{:S(2)}, u32[]{:S(2)}) collective-permute-start(bf16[2,96,576]{2,1,0:T(8,128)(2,1)} %slice.133), channel_id=1, source_target_pairs={{0,3},{1,0},{2,1},{3,2},{4,7},{5,4},{6,5},{7,6},{8,11},{9,8},{10,9... | collective-permute-start | bytes 663560 | tf_op jit(solution)/shard_map/ppermute | solution.py:44
  47.0 0.7 slice.134
  47.7 6.7 %collective-permute-done.5 = bf16[4,96,576]{2,1,0:T(8,128)(2,1)S(1)} collective-permute-done((bf16[4,96,576]{2,1,0:T(8,128)(2,1)S(1)}, bf16[4,96,576]{2,1,0:T(8,128)(2,1)S(1)}, u32[]{:S(2)}, u32[]{:S(2)}) %collective-permute-start.5) | collective-permute-done | bytes 442400 | tf_op jit(solution)/shard_map/ppermute | solution.py:42
  54.4 0.7 slice.131
  55.1 3.5 %collective-permute-start.7 = (bf16[2,96,576]{2,1,0:T(8,128)(2,1)}, bf16[2,96,576]{2,1,0:T(8,128)(2,1)}, u32[]{:S(2)}, u32[]{:S(2)}) collective-permute-start(bf16[2,96,576]{2,1,0:T(8,128)(2,1)} %slice.131), channel_id=1, source_target_pairs={{0,12},{1,13},{2,14},{3,15},{4,0},{5,1},{6,2},{7,3},{8,4},{9,5},{1... | collective-permute-start | bytes 663560 | tf_op jit(solution)/shard_map/ppermute | solution.py:44
  58.7 0.7 slice.132
  59.4 0.8 copy-done.1
  60.4 3.2 %collective-permute-done.7 = bf16[2,96,576]{2,1,0:T(8,128)(2,1)} collective-permute-done((bf16[2,96,576]{2,1,0:T(8,128)(2,1)}, bf16[2,96,576]{2,1,0:T(8,128)(2,1)}, u32[]{:S(2)}, u32[]{:S(2)}) %collective-permute-start.7) | collective-permute-done | bytes 221216 | tf_op jit(solution)/shard_map/ppermute | solution.py:44
  63.6 4.6 %collective-permute-done.8 = bf16[2,96,576]{2,1,0:T(8,128)(2,1)} collective-permute-done((bf16[2,96,576]{2,1,0:T(8,128)(2,1)}, bf16[2,96,576]{2,1,0:T(8,128)(2,1)}, u32[]{:S(2)}, u32[]{:S(2)}) %collective-permute-start.8) | collective-permute-done | bytes 221216 | tf_op jit(solution)/shard_map/ppermute | solution.py:45
  68.2 1.0 copy-done.2
  69.2 4.2 %shard_map.100 = (bf16[2,2,64,384]{3,2,1,0:T(8,128)(2,1)S(1)}, bf16[2,64,384]{2,1,0:T(8,128)(2,1)S(1)}) custom-call(s32[1]{0:T(128)} %bitcast.3.core_ref, bf16[128,3072]{1,0:T(8,128)(2,1)S(1)} %bitcast.54, bf16[128,3072]{1,0:T(8,128)(2,1)} %collective-permute-done.1.other_ref, f32[2,128]{1,0:T(2,128)S(1)} %pad_maximum_fusion.5.gain_ref, ...), custom_call_target="tpu_custom_call" | custom-call | flops 905969664 | bytes 3538944 | tf_op jit(solution)/shard_map/pallas_call | solution.py:124
  73.4 1.0 broadcast_in_dim.9
  74.4 3.9 %all-to-all-start.1 = ((bf16[16,64,384]{2,1,0:T(8,128)(2,1)}), bf16[16,64,384]{2,1,0:T(8,128)(2,1)S(1)}, u32[]{:S(2)}, u32[]{:S(2)}) async-start(bf16[16,64,384]{2,1,0:T(8,128)(2,1)} %bitcast.31), calls=%async_computation.1 | async-start | bytes 1572864 | tf_op jit(solution)/shard_map/all_to_all | solution.py:300
  78.4 12.3 %all-to-all-done.1 = bf16[16,64,384]{2,1,0:T(8,128)(2,1)S(1)} async-done(((bf16[16,64,384]{2,1,0:T(8,128)(2,1)}), bf16[16,64,384]{2,1,0:T(8,128)(2,1)S(1)}, u32[]{:S(2)}, u32[]{:S(2)}) %all-to-all-start.1) | async-done | bytes 786464 | tf_op jit(solution)/shard_map/all_to_all | solution.py:300
  90.6 1.1 broadcast_in_dim.10
  91.7 3.7 %all-to-all-start.2 = ((bf16[16,24,1536]{2,1,0:T(8,128)(2,1)}), bf16[16,24,1536]{2,1,0:T(8,128)(2,1)S(1)}, u32[]{:S(2)}, u32[]{:S(2)}) async-start(bf16[16,24,1536]{2,1,0:T(8,128)(2,1)} %broadcast_in_dim.10), calls=%async_computation.2 | async-start | bytes 2359296 | tf_op jit(solution)/shard_map/all_to_all | solution.py:311
  95.4 3.2 %collective-permute-start.18 = (bf16[1024,384]{1,0:T(8,128)(2,1)S(1)}, bf16[1024,384]{1,0:T(8,128)(2,1)S(1)}, u32[]{:S(2)}, u32[]{:S(2)}) collective-permute-start(bf16[1024,384]{1,0:T(8,128)(2,1)S(1)} %bitcast.61), channel_id=1, source_target_pairs={{0,128},{128,0},{1,129},{129,1},{2,130},{130,2},{3,131},{131,3},{4... | collective-permute-start | bytes 2359304 | tf_op jit(solution)/shard_map/ppermute | solution.py:302
  98.7 3.3 %collective-permute-start.16 = (bf16[64,384]{1,0:T(8,128)(2,1)S(1)}, bf16[64,384]{1,0:T(8,128)(2,1)S(1)}, u32[]{:S(2)}, u32[]{:S(2)}) collective-permute-start(bf16[64,384]{1,0:T(8,128)(2,1)S(1)} %get-tuple-element.32), channel_id=1, source_target_pairs={{0,0},{1,1},{4,128},{5,129},{128,4},{129,5},{132,132},{133,133},{2... | collective-permute-start | bytes 147464 | tf_op jit(solution)/shard_map/ppermute | solution.py:306
  101.9 1.6 %collective-permute-start.17 = (bf16[64,384]{1,0:T(8,128)(2,1)S(1)}, bf16[64,384]{1,0:T(8,128)(2,1)S(1)}, u32[]{:S(2)}, u32[]{:S(2)}) collective-permute-start(bf16[64,384]{1,0:T(8,128)(2,1)S(1)} %get-tuple-element.31), channel_id=1, source_target_pairs={{0,1},{1,0},{4,129},{5,128},{128,5},{129,4},{132,133},{133,132},{2... | collective-permute-start | bytes 147464 | tf_op jit(solution)/shard_map/ppermute | solution.py:307
  103.6 8.7 %collective-permute-done.16.q0_ref = bf16[64,384]{1,0:T(8,128)(2,1)S(1)} collective-permute-done((bf16[64,384]{1,0:T(8,128)(2,1)S(1)}, bf16[64,384]{1,0:T(8,128)(2,1)S(1)}, u32[]{:S(2)}, u32[]{:S(2)}) %collective-permute-start.16) | collective-permute-done | bytes 49184 | tf_op jit(solution)/shard_map/ppermute | solution.py:306
  112.3 0.7 collective-permute-done.17.q1_ref
  113.0 2.9 %shard_map.101 = (bf16[64,384]{1,0:T(8,128)(2,1)S(1)}, bf16[64,384]{1,0:T(8,128)(2,1)S(1)}) custom-call(s32[1]{0:T(128)} %bitcast.3.core_ref, bf16[64,384]{1,0:T(8,128)(2,1)S(1)} %collective-permute-done.16.q0_ref, bf16[64,384]{1,0:T(8,128)(2,1)S(1)} %collective-permute-done.17.q1_ref, bf16[1024,384]{1,0:T(8,128)(2,1)S(1)} %bitcast.62, ...), custom_call_target="tpu_custom_call" | custom-call | flops 805306368 | bytes 1572864 | tf_op jit(solution)/shard_map/pallas_call | solution.py:188
  115.8 1.9 %collective-permute-start.19 = (bf16[64,384]{1,0:T(8,128)(2,1)S(1)}, bf16[64,384]{1,0:T(8,128)(2,1)S(1)}, u32[]{:S(2)}, u32[]{:S(2)}) collective-permute-start(bf16[64,384]{1,0:T(8,128)(2,1)S(1)} %get-tuple-element.14), channel_id=1, source_target_pairs={{0,0},{1,1},{4,128},{5,129},{128,4},{129,5},{132,132},{133,133},{2... | collective-permute-start | bytes 147464 | tf_op jit(solution)/shard_map/ppermute | solution.py:318
  117.9 2.0 %collective-permute-start.21 = (bf16[64,384]{1,0:T(8,128)(2,1)S(1)}, bf16[64,384]{1,0:T(8,128)(2,1)S(1)}, u32[]{:S(2)}, u32[]{:S(2)}) collective-permute-start(bf16[64,384]{1,0:T(8,128)(2,1)S(1)} %get-tuple-element.15), channel_id=1, source_target_pairs={{0,1},{1,0},{4,129},{5,128},{128,5},{129,4},{132,133},{133,132},{2... | collective-permute-start | bytes 147464 | tf_op jit(solution)/shard_map/ppermute | solution.py:318
  119.9 1.0 collective-permute-start.22
  121.0 0.6 collective-permute-done.19.p00_ref
  121.6 1.3 collective-permute-done.21.p10_ref
  122.9 0.8 collective-permute-done.22.p11_ref
  123.7 2.1 %shard_map.102 = bf16[8,32,1536]{2,1,0:T(8,128)(2,1)} custom-call(s32[2]{0:T(128)S(1)} %pad_add_fusion.1.bits_ref, bf16[64,384]{1,0:T(8,128)(2,1)S(1)} %collective-permute-done.19.p00_ref, bf16[64,384]{1,0:T(8,128)(2,1)S(1)} %collective-permute-done.20.p01_ref, bf16[64,384]{1,0:T(8,128)(2,1)S(1)} %collective-permute-done.21.p10_ref, ...), custom_call_target="tpu_custom_call" | custom-call | flops 301989888 | bytes 1179648 | tf_op jit(solution)/shard_map/pallas_call | solution.py:238
  125.8 3.7 %all-to-all-start.3 = ((bf16[8,32,1536]{2,1,0:T(8,128)(2,1)}), bf16[8,32,1536]{2,1,0:T(8,128)(2,1)S(1)}, u32[]{:S(2)}, u32[]{:S(2)}) async-start(bf16[8,32,1536]{2,1,0:T(8,128)(2,1)} %shard_map.102), calls=%async_computation.3 | async-start | bytes 1572864 | tf_op jit(solution)/shard_map/all_to_all | solution.py:323
  130.2 1.0 collective-permute-start
  131.1 0.8 collective-permute-done
  132.0 0.6 fusion.17
  140.2 0.6 fusion.16
  140.8 1.0 dynamic-slice_reduce_fusion.2
  141.8 11.1 %all-to-all-done.3 = bf16[8,32,1536]{2,1,0:T(8,128)(2,1)S(1)} async-done(((bf16[8,32,1536]{2,1,0:T(8,128)(2,1)}), bf16[8,32,1536]{2,1,0:T(8,128)(2,1)S(1)}, u32[]{:S(2)}, u32[]{:S(2)}) %all-to-all-start.3) | async-done | bytes 786464 | tf_op jit(solution)/shard_map/all_to_all | solution.py:323
  153.1 1.3 add_select_fusion.1
  154.4 0.6 collective-permute-start.23
  154.9 0.9 collective-permute-done.23
  155.9 0.7 fusion.5
  (64 shorter events, 1.8 us)
Async XLA Ops:
  0.0 78.4 %copy-start = (bf16[24,3072]{1,0:T(8,128)(2,1)S(1)}, bf16[24,3072]{1,0:T(8,128)(2,1)}, u32[]{:S(2)}) copy-start(bf16[24,3072]{1,0:T(8,128)(2,1)} %param.13) | copy-start | bytes 442372
  5.5 11.3 %copy-start.3 = (bf16[192,3,384]{2,0,1:T(8,128)(2,1)S(1)}, bf16[192,3,384]{2,0,1:T(8,128)(2,1)}, u32[]{:S(2)}) copy-start(bf16[192,3,384]{2,0,1:T(8,128)(2,1)} %param.12) | copy-start | bytes 1327108
  7.8 32.6 %all-to-all-start = ((bf16[8,16,3072]{2,1,0:T(8,128)(2,1)}), bf16[8,16,3072]{2,1,0:T(8,128)(2,1)S(1)}, u32[]{:S(2)}, u32[]{:S(2)}) async-start(bf16[8,16,3072]{2,1,0:T(8,128)(2,1)} %broadcast_in_dim.8), calls=%async_computation | async-start | bytes 1572864 | tf_op jit(solution)/shard_map/all_to_all | solution.py:280
  17.0 43.2 %copy-start.6 = (f32[64]{0:T(128)S(1)}, f32[64]{0:T(128)}, u32[]{:S(2)}) copy-start(f32[64]{0:T(128)} %param.14) | copy-start | bytes 772
  17.0 43.3 %copy-start.7 = (f32[64]{0:T(128)S(1)}, f32[64]{0:T(128)}, u32[]{:S(2)}) copy-start(f32[64]{0:T(128)} %param.15) | copy-start | bytes 772
  17.0 6.9 %collective-permute-start.9 = (bf16[96,576]{1,0:T(8,128)(2,1)S(1)}, bf16[96,576]{1,0:T(8,128)(2,1)S(1)}, u32[]{:S(2)}, u32[]{:S(2)}) collective-permute-start(bf16[96,576]{1,0:T(8,128)(2,1)S(1)} %get-tuple-element.23), channel_id=1, source_target_pairs={{0,12},{1,13},{2,14},{3,15},{4,0},{5,1},{6,2},{7,3},{8,4},{9,5},{1... | collective-permute-start | bytes 331784 | tf_op jit(solution)/shard_map/ppermute | solution.py:35
  19.9 5.5 %collective-permute-start.10 = (bf16[96,576]{1,0:T(8,128)(2,1)S(1)}, bf16[96,576]{1,0:T(8,128)(2,1)S(1)}, u32[]{:S(2)}, u32[]{:S(2)}) collective-permute-start(bf16[96,576]{1,0:T(8,128)(2,1)S(1)} %get-tuple-element.23), channel_id=1, source_target_pairs={{0,8},{1,9},{2,10},{3,11},{4,12},{5,13},{6,14},{7,15},{8,0},{9,1},... | collective-permute-start | bytes 331784 | tf_op jit(solution)/shard_map/ppermute | solution.py:37
  20.2 8.5 %collective-permute-start.11 = (bf16[96,576]{1,0:T(8,128)(2,1)S(1)}, bf16[96,576]{1,0:T(8,128)(2,1)S(1)}, u32[]{:S(2)}, u32[]{:S(2)}) collective-permute-start(bf16[96,576]{1,0:T(8,128)(2,1)S(1)} %get-tuple-element.23), channel_id=1, source_target_pairs={{0,4},{1,5},{2,6},{3,7},{4,8},{5,9},{6,10},{7,11},{8,12},{9,13},{1... | collective-permute-start | bytes 331784 | tf_op jit(solution)/shard_map/ppermute | solution.py:36
  20.9 10.5 %collective-permute-start.2 = (bf16[96,576]{1,0:T(8,128)(2,1)S(1)}, bf16[96,576]{1,0:T(8,128)(2,1)S(1)}, u32[]{:S(2)}, u32[]{:S(2)}) collective-permute-start(bf16[96,576]{1,0:T(8,128)(2,1)S(1)} %get-tuple-element.24), channel_id=1, source_target_pairs={{0,3},{1,0},{2,1},{3,2},{4,7},{5,4},{6,5},{7,6},{8,11},{9,8},{10,9... | collective-permute-start | bytes 331784 | tf_op jit(solution)/shard_map/ppermute | solution.py:35
  23.4 17.5 %collective-permute-start.3 = (bf16[96,576]{1,0:T(8,128)(2,1)S(1)}, bf16[96,576]{1,0:T(8,128)(2,1)S(1)}, u32[]{:S(2)}, u32[]{:S(2)}) collective-permute-start(bf16[96,576]{1,0:T(8,128)(2,1)S(1)} %get-tuple-element.24), channel_id=1, source_target_pairs={{0,2},{1,3},{2,0},{3,1},{4,6},{5,7},{6,4},{7,5},{8,10},{9,11},{10,... | collective-permute-start | bytes 331784 | tf_op jit(solution)/shard_map/ppermute | solution.py:37
  23.9 17.0 %collective-permute-start.4 = (bf16[96,576]{1,0:T(8,128)(2,1)S(1)}, bf16[96,576]{1,0:T(8,128)(2,1)S(1)}, u32[]{:S(2)}, u32[]{:S(2)}) collective-permute-start(bf16[96,576]{1,0:T(8,128)(2,1)S(1)} %get-tuple-element.24), channel_id=1, source_target_pairs={{0,1},{1,2},{2,3},{3,0},{4,5},{5,6},{6,7},{7,4},{8,9},{9,10},{10,1... | collective-permute-start | bytes 331784 | tf_op jit(solution)/shard_map/ppermute | solution.py:36
  28.8 15.0 %collective-permute-start.12 = (bf16[4,96,576]{2,1,0:T(8,128)(2,1)S(1)}, bf16[4,96,576]{2,1,0:T(8,128)(2,1)S(1)}, u32[]{:S(2)}, u32[]{:S(2)}) collective-permute-start(bf16[4,96,576]{2,1,0:T(8,128)(2,1)S(1)} %pad_maximum_fusion.1), channel_id=1, source_target_pairs={{0,3},{1,0},{2,1},{3,2},{4,7},{5,4},{6,5},{7,6},{8,11},{9,8},{10,9... | collective-permute-start | bytes 1327112 | tf_op jit(solution)/shard_map/ppermute | solution.py:42
  31.3 15.6 %collective-permute-start.13 = (bf16[4,96,576]{2,1,0:T(8,128)(2,1)S(1)}, bf16[4,96,576]{2,1,0:T(8,128)(2,1)S(1)}, u32[]{:S(2)}, u32[]{:S(2)}) collective-permute-start(bf16[4,96,576]{2,1,0:T(8,128)(2,1)S(1)} %pad_maximum_fusion.1), channel_id=1, source_target_pairs={{0,1},{1,2},{2,3},{3,0},{4,5},{5,6},{6,7},{7,4},{8,9},{9,10},{10,1... | collective-permute-start | bytes 1327112 | tf_op jit(solution)/shard_map/ppermute | solution.py:43
  40.4 27.8 %collective-permute-start.1 = (bf16[128,3072]{1,0:T(8,128)(2,1)S(1)}, bf16[128,3072]{1,0:T(8,128)(2,1)}, u32[]{:S(2)}, u32[]{:S(2)}) collective-permute-start(bf16[128,3072]{1,0:T(8,128)(2,1)S(1)} %bitcast.53), channel_id=1, source_target_pairs={{0,128},{128,0},{1,129},{129,1},{2,130},{130,2},{3,131},{131,3},{4... | collective-permute-start | bytes 2359304 | tf_op jit(solution)/shard_map/ppermute | solution.py:283
  41.0 13.5 %collective-permute-start.5 = (bf16[4,96,576]{2,1,0:T(8,128)(2,1)S(1)}, bf16[4,96,576]{2,1,0:T(8,128)(2,1)S(1)}, u32[]{:S(2)}, u32[]{:S(2)}) collective-permute-start(bf16[4,96,576]{2,1,0:T(8,128)(2,1)S(1)} %pad_maximum_fusion), channel_id=1, source_target_pairs={{0,12},{1,13},{2,14},{3,15},{4,0},{5,1},{6,2},{7,3},{8,4},{9,5},{1... | collective-permute-start | bytes 1327112 | tf_op jit(solution)/shard_map/ppermute | solution.py:42
  43.8 14.9 %collective-permute-start.6 = (bf16[4,96,576]{2,1,0:T(8,128)(2,1)S(1)}, bf16[4,96,576]{2,1,0:T(8,128)(2,1)S(1)}, u32[]{:S(2)}, u32[]{:S(2)}) collective-permute-start(bf16[4,96,576]{2,1,0:T(8,128)(2,1)S(1)} %pad_maximum_fusion), channel_id=1, source_target_pairs={{0,4},{1,5},{2,6},{3,7},{4,8},{5,9},{6,10},{7,11},{8,12},{9,13},{1... | collective-permute-start | bytes 1327112 | tf_op jit(solution)/shard_map/ppermute | solution.py:43
  44.5 15.9 %collective-permute-start.14 = (bf16[2,96,576]{2,1,0:T(8,128)(2,1)}, bf16[2,96,576]{2,1,0:T(8,128)(2,1)}, u32[]{:S(2)}, u32[]{:S(2)}) collective-permute-start(bf16[2,96,576]{2,1,0:T(8,128)(2,1)} %slice.133), channel_id=1, source_target_pairs={{0,3},{1,0},{2,1},{3,2},{4,7},{5,4},{6,5},{7,6},{8,11},{9,8},{10,9... | collective-permute-start | bytes 663560 | tf_op jit(solution)/shard_map/ppermute | solution.py:44
  47.7 12.7 %collective-permute-start.15 = (bf16[2,96,576]{2,1,0:T(8,128)(2,1)}, bf16[2,96,576]{2,1,0:T(8,128)(2,1)}, u32[]{:S(2)}, u32[]{:S(2)}) collective-permute-start(bf16[2,96,576]{2,1,0:T(8,128)(2,1)} %slice.134), channel_id=1, source_target_pairs={{0,1},{1,2},{2,3},{3,0},{4,5},{5,6},{6,7},{7,4},{8,9},{9,10},{10,1... | collective-permute-start | bytes 663560 | tf_op jit(solution)/shard_map/ppermute | solution.py:45
  55.1 8.4 %collective-permute-start.7 = (bf16[2,96,576]{2,1,0:T(8,128)(2,1)}, bf16[2,96,576]{2,1,0:T(8,128)(2,1)}, u32[]{:S(2)}, u32[]{:S(2)}) collective-permute-start(bf16[2,96,576]{2,1,0:T(8,128)(2,1)} %slice.131), channel_id=1, source_target_pairs={{0,12},{1,13},{2,14},{3,15},{4,0},{5,1},{6,2},{7,3},{8,4},{9,5},{1... | collective-permute-start | bytes 663560 | tf_op jit(solution)/shard_map/ppermute | solution.py:44
  59.4 0.8 copy-start.1
  60.2 8.0 %collective-permute-start.8 = (bf16[2,96,576]{2,1,0:T(8,128)(2,1)}, bf16[2,96,576]{2,1,0:T(8,128)(2,1)}, u32[]{:S(2)}, u32[]{:S(2)}) collective-permute-start(bf16[2,96,576]{2,1,0:T(8,128)(2,1)} %slice.132), channel_id=1, source_target_pairs={{0,4},{1,5},{2,6},{3,7},{4,8},{5,9},{6,10},{7,11},{8,12},{9,13},{1... | collective-permute-start | bytes 663560 | tf_op jit(solution)/shard_map/ppermute | solution.py:45
  68.2 1.0 copy-start.2
  74.4 16.2 %all-to-all-start.1 = ((bf16[16,64,384]{2,1,0:T(8,128)(2,1)}), bf16[16,64,384]{2,1,0:T(8,128)(2,1)S(1)}, u32[]{:S(2)}, u32[]{:S(2)}) async-start(bf16[16,64,384]{2,1,0:T(8,128)(2,1)} %bitcast.31), calls=%async_computation.1 | async-start | bytes 1572864 | tf_op jit(solution)/shard_map/all_to_all | solution.py:300
  91.7 32.0 %all-to-all-start.2 = ((bf16[16,24,1536]{2,1,0:T(8,128)(2,1)}), bf16[16,24,1536]{2,1,0:T(8,128)(2,1)S(1)}, u32[]{:S(2)}, u32[]{:S(2)}) async-start(bf16[16,24,1536]{2,1,0:T(8,128)(2,1)} %broadcast_in_dim.10), calls=%async_computation.2 | async-start | bytes 2359296 | tf_op jit(solution)/shard_map/all_to_all | solution.py:311
  95.4 17.5 %collective-permute-start.18 = (bf16[1024,384]{1,0:T(8,128)(2,1)S(1)}, bf16[1024,384]{1,0:T(8,128)(2,1)S(1)}, u32[]{:S(2)}, u32[]{:S(2)}) collective-permute-start(bf16[1024,384]{1,0:T(8,128)(2,1)S(1)} %bitcast.61), channel_id=1, source_target_pairs={{0,128},{128,0},{1,129},{129,1},{2,130},{130,2},{3,131},{131,3},{4... | collective-permute-start | bytes 2359304 | tf_op jit(solution)/shard_map/ppermute | solution.py:302
  98.7 13.6 %collective-permute-start.16 = (bf16[64,384]{1,0:T(8,128)(2,1)S(1)}, bf16[64,384]{1,0:T(8,128)(2,1)S(1)}, u32[]{:S(2)}, u32[]{:S(2)}) collective-permute-start(bf16[64,384]{1,0:T(8,128)(2,1)S(1)} %get-tuple-element.32), channel_id=1, source_target_pairs={{0,0},{1,1},{4,128},{5,129},{128,4},{129,5},{132,132},{133,133},{2... | collective-permute-start | bytes 147464 | tf_op jit(solution)/shard_map/ppermute | solution.py:306
  101.9 11.0 %collective-permute-start.17 = (bf16[64,384]{1,0:T(8,128)(2,1)S(1)}, bf16[64,384]{1,0:T(8,128)(2,1)S(1)}, u32[]{:S(2)}, u32[]{:S(2)}) collective-permute-start(bf16[64,384]{1,0:T(8,128)(2,1)S(1)} %get-tuple-element.31), channel_id=1, source_target_pairs={{0,1},{1,0},{4,129},{5,128},{128,5},{129,4},{132,133},{133,132},{2... | collective-permute-start | bytes 147464 | tf_op jit(solution)/shard_map/ppermute | solution.py:307
  115.8 24.4 %copy-start.5 = (f32[50]{0:T(128)S(1)}, f32[50]{0:T(128)}, u32[]{:S(2)}) copy-start(f32[50]{0:T(128)} %param.18) | copy-start | bytes 604
  115.8 5.7 %collective-permute-start.19 = (bf16[64,384]{1,0:T(8,128)(2,1)S(1)}, bf16[64,384]{1,0:T(8,128)(2,1)S(1)}, u32[]{:S(2)}, u32[]{:S(2)}) collective-permute-start(bf16[64,384]{1,0:T(8,128)(2,1)S(1)} %get-tuple-element.14), channel_id=1, source_target_pairs={{0,0},{1,1},{4,128},{5,129},{128,4},{129,5},{132,132},{133,133},{2... | collective-permute-start | bytes 147464 | tf_op jit(solution)/shard_map/ppermute | solution.py:318
  117.8 3.8 %collective-permute-start.20 = (bf16[64,384]{1,0:T(8,128)(2,1)S(1)}, bf16[64,384]{1,0:T(8,128)(2,1)S(1)}, u32[]{:S(2)}, u32[]{:S(2)}) collective-permute-start(bf16[64,384]{1,0:T(8,128)(2,1)S(1)} %get-tuple-element.14), channel_id=1, source_target_pairs={{0,128},{1,129},{4,0},{5,1},{128,132},{129,133},{132,4},{133,5},{2... | collective-permute-start | bytes 147464 | tf_op jit(solution)/shard_map/ppermute | solution.py:318
  117.9 5.0 %collective-permute-start.21 = (bf16[64,384]{1,0:T(8,128)(2,1)S(1)}, bf16[64,384]{1,0:T(8,128)(2,1)S(1)}, u32[]{:S(2)}, u32[]{:S(2)}) collective-permute-start(bf16[64,384]{1,0:T(8,128)(2,1)S(1)} %get-tuple-element.15), channel_id=1, source_target_pairs={{0,1},{1,0},{4,129},{5,128},{128,5},{129,4},{132,133},{133,132},{2... | collective-permute-start | bytes 147464 | tf_op jit(solution)/shard_map/ppermute | solution.py:318
  119.9 3.8 %collective-permute-start.22 = (bf16[64,384]{1,0:T(8,128)(2,1)S(1)}, bf16[64,384]{1,0:T(8,128)(2,1)S(1)}, u32[]{:S(2)}, u32[]{:S(2)}) collective-permute-start(bf16[64,384]{1,0:T(8,128)(2,1)S(1)} %get-tuple-element.15), channel_id=1, source_target_pairs={{0,129},{1,128},{4,1},{5,0},{128,133},{129,132},{132,5},{133,4},{2... | collective-permute-start | bytes 147464 | tf_op jit(solution)/shard_map/ppermute | solution.py:318
  125.8 30.1 %copy-start.4 = (f32[16,3072]{1,0:T(8,128)S(1)}, f32[16,3072]{1,0:T(8,128)}, u32[]{:S(2)}) copy-start(f32[16,3072]{1,0:T(8,128)} %param.11) | copy-start | bytes 589828
  125.8 27.2 %all-to-all-start.3 = ((bf16[8,32,1536]{2,1,0:T(8,128)(2,1)}), bf16[8,32,1536]{2,1,0:T(8,128)(2,1)S(1)}, u32[]{:S(2)}, u32[]{:S(2)}) async-start(bf16[8,32,1536]{2,1,0:T(8,128)(2,1)} %shard_map.102), calls=%async_computation.3 | async-start | bytes 1572864 | tf_op jit(solution)/shard_map/all_to_all | solution.py:323
  130.2 1.8 %collective-permute-start = (s32[2]{0:T(128)S(1)}, s32[2]{0:T(128)S(1)}, u32[]{:S(2)}, u32[]{:S(2)}) collective-permute-start(s32[2]{0:T(128)S(1)} %pad_add_fusion), channel_id=1, source_target_pairs={{0,128},{128,0},{1,129},{129,1},{2,130},{130,2},{3,131},{131,3},{4... | collective-permute-start | bytes 32 | tf_op jit(solution)/shard_map/ppermute | solution.py:327
  154.4 1.5 collective-permute-start.23
